TPU v7x, 32 devices: a whole 2x2x4 slice. The times are simulated.
32 devices in a mesh: groups: 2 (over x), chan: 8 (over z, y), seq: 2 (over core).
Axes of the slice: x: 2, y: 2, z: 4, core: 2. Of those that a mesh axis runs over, the one named last changes fastest.
Arguments:
- tokens: bfloat16 [2048, 8192], P(('groups', 'seq'), 'chan'), parts along dimension 0, may hold values from -42 to 42
- norm_gain: float32 [8192], replicated, may hold values from 0.1 to 1.9
- in_weight: bfloat16 [3, 8192, 8192], P(None, None, 'chan'), may hold values from -0.0625 to 0.0625
- short_weight: float32 [3, 7, 8192], P(None, None, 'chan'), may hold values from -2 to 2
- log_decay: float32 [16, 8192], P(None, 'chan'), may hold values from -0.034 to 0
- residue: float32 [16, 8192], P(None, 'chan'), may hold values from -0.15625 to 0.15625
- skip: float32 [8192], P('chan'), may hold values from 0.1 to 1.9
- out_weight: bfloat16 [8192, 8192], P('chan'), may hold values from -0.09375 to 0.09375
Outputs:
- mixed: bfloat16 [2048, 8192], P(('groups', 'seq'), 'chan'), parts along dimension 0
There are 2 independent parts, one for each index of `groups`. A program takes and returns all parts, laid end to end along the dimension named above; an argument that names none is the same for every part. Nothing has to cross between parts.
All inputs are finite; a program needn't handle non-finite values.
Results may differ from a plain program's by a relative error of at most 0.0067.
Values may be sent and summed in bfloat16 or wider, within the bound.
No kernel may reach another device: no remote copies, remote signals or barrier semaphores. Data moves between devices by JAX's collectives and lax.ppermute only.
A program may use at most 448 MiB of HBM per device.

v0:
```python
import jax
import jax.numpy as jnp
from jax import lax
from jax.sharding import PartitionSpec as P

EPSILON = 1e-06


def from_behind(block, axis, distance):
    devices = range(lax.axis_size(axis))
    route = [(i - distance, i) for i in devices if i - distance in devices]
    return lax.ppermute(block, axis, route)


def prefix(part, axis, combine, identity):
    place = lax.axis_index(axis)
    gathered = jax.tree.map(lambda a: lax.all_gather(a, axis), part)
    state = jax.tree.map(lambda a, e: jnp.zeros_like(a) + jnp.asarray(e, a.dtype), part, identity)

    def one(step, state):
        return combine(
            state, jax.tree.map(lambda a: lax.dynamic_index_in_dim(a, step, 0, False), gathered)
        )

    return lax.fori_loop(0, place, one, state)


def scan_pair(earlier, later):
    return (earlier[0] * later[0], earlier[1] * later[0] + later[1])


def per_device(tokens, norm_gain, in_weight, short_weight, log_decay, residue, skip, out_weight):
    tok_count = tokens.shape[0]
    chan_width = tokens.shape[1]
    model_width = norm_gain.shape[0]
    tap_count = short_weight.shape[1]
    tok_float = tokens.astype(jnp.float32)
    squares = lax.psum(jnp.sum(tok_float * tok_float, axis=1), "chan")
    inv_rms = lax.rsqrt(squares / model_width + EPSILON)[:, None]
    scaled = (
        lax.all_gather(tokens, "chan", axis=1, tiled=True).astype(jnp.float32) * norm_gain[None, :]
    ).astype(jnp.bfloat16)
    projected = jnp.einsum("td,kdc->ktc", scaled, in_weight, preferred_element_type=jnp.float32)
    proj = (projected * inv_rms[None]).astype(jnp.bfloat16)
    rim_rows = proj[:, tok_count - (tap_count - 1) :, :]
    earlier_rows = from_behind(rim_rows, "seq", 1)
    extended = jnp.concatenate([earlier_rows, proj], axis=1).astype(jnp.float32)
    conv = jnp.zeros((3, tok_count, chan_width), jnp.float32)
    for tap in range(tap_count):
        conv = (
            conv
            + short_weight[:, tap][:, None, :]
            * extended[:, tap_count - 1 - tap : tap_count - 1 - tap + tok_count, :]
        )
    query = conv[0]
    product = conv[1] * conv[2]
    blk_size = min(128, tok_count)
    blk_count = tok_count // blk_size
    positions = jnp.arange(blk_size, dtype=jnp.float32)
    pole_power = jnp.exp(positions[:, None, None] * log_decay[None])
    weighted = pole_power * residue[None]
    filt_rows = jnp.sum(weighted, axis=1).T
    padded_filt = jnp.concatenate(
        [filt_rows[:, :1], jnp.zeros((chan_width, blk_size), jnp.float32), filt_rows[:, :0:-1]],
        axis=1,
    )
    tiled = jnp.tile(padded_filt, (1, blk_size))[:, : blk_size * (2 * blk_size - 1)]
    toeplitz = tiled.reshape(chan_width, blk_size, 2 * blk_size - 1)[:, :, :blk_size]
    product_blocks = product.reshape(blk_count, blk_size, chan_width)
    inner_part = jnp.einsum(
        "cts,ksc->ktc", toeplitz, product_blocks, precision=lax.Precision.HIGHEST
    )
    back_power = jnp.exp((blk_size - positions)[:, None, None] * log_decay[None])
    block_states = jnp.einsum(
        "ksc,snc->knc", product_blocks, back_power, precision=lax.Precision.HIGHEST
    )
    block_decay = jnp.exp(blk_size * log_decay)
    carried = jnp.zeros_like(log_decay)
    entering = []
    for span_idx in range(blk_count):
        entering.append(carried)
        carried = block_decay * carried + block_states[span_idx]
    shard_decay = jnp.exp(tok_count * log_decay)
    unused_decay, state_in = prefix(
        (shard_decay, carried),
        "seq",
        scan_pair,
        (jnp.ones_like(log_decay), jnp.zeros_like(log_decay)),
    )
    span_starts = jnp.arange(blk_count, dtype=jnp.float32) * blk_size
    lead_decay = jnp.exp(span_starts[:, None, None] * log_decay[None])
    entry_states = lead_decay * state_in[None] + jnp.stack(entering)
    carry_part = jnp.einsum("tnc,knc->ktc", weighted, entry_states, precision=lax.Precision.HIGHEST)
    long_conv = (inner_part + carry_part).reshape(tok_count, chan_width)
    gated = (query * (long_conv + skip[None, :] * product)).astype(jnp.bfloat16)
    partial_sums = jnp.dot(gated, out_weight, preferred_element_type=jnp.float32)
    branch_out = lax.psum_scatter(partial_sums, "chan", scatter_dimension=1, tiled=True)
    return (tok_float + branch_out).astype(jnp.bfloat16)


def solution(mesh):
    return jax.shard_map(
        per_device,
        mesh=mesh,
        in_specs=(
            P(("groups", "seq"), "chan"),
            P(),
            P(None, None, "chan"),
            P(None, None, "chan"),
            P(None, "chan"),
            P(None, "chan"),
            P("chan"),
            P("chan", None),
        ),
        out_specs=P(("groups", "seq"), "chan"),
        check_vma=False,
    )
```

profile of v0, /device:TPU:0, one launch (start us, length us, event | category | flops | bytes accessed | tf_op | source)
XLA Modules:
  0.0 1114.5 jit_solution(7528255123943374717)
XLA Ops:
  6.5 0.7 all-gather.4.cloned.1.call-update
  7.3 1.0 copy.56
  8.4 1.1 copy.55
  9.5 11.7 %fusion.9 = f32[128,1024]{0,1:T(8,128)S(1)} fusion(f32[16,1024]{0,1:T(8,128)S(1)} %copy.56, f32[16,1024]{0,1:T(8,128)S(1)} %copy.55), kind=kLoop, calls=%fused_computation.12 | loop fusion | flops 6160384 | bytes 655360 | tf_op jit(solution)/shard_map/reduce_sum | solution.py:62
  21.4 0.7 rev.3
  22.5 23.8 %psum.7 = f32[512]{0:T(512)S(1)} all-reduce(f32[512]{0:T(512)S(1)} %fusion.22), channel_id=1, replica_groups=mesh['groups'=2,'chan'=8,'seq'=2] {'chan'}, use_global_device_ids=true, to_apply=%region_1.0 | all-reduce | flops 512 | bytes 4096 | tf_op jit(solution)/shard_map/psum | solution.py:38
  49.0 88.5 %all-gather.4.cloned.1.call-done = bf16[512,8192]{1,0:T(8,128)(2,1)} async-done(((bf16[512,1024]{1,0:T(8,128)(2,1)}), bf16[512,8192]{1,0:T(8,128)(2,1)}) %all-gather.4.cloned.1.call-update) | async-done | bytes 8388624 | tf_op jit(solution)/shard_map/all_gather | solution.py:41
  137.5 33.8 %fusion.21 = bf16[3,512,1024]{2,1,0:T(8,128)(2,1)S(1)} fusion(f32[512]{0:T(512)S(1)} %add_rsqrt_fusion, bf16[3,8192,1024]{2,1,0:T(8,128)(2,1)} %param.12, bf16[512,8192]{1,0:T(8,128)(2,1)} %all-gather.4.cloned.1.call-done, f32[8192]{0:T(1024)S(1)} %copy-done.20), kind=kOutput, calls=%fused_computation.33 | convolution fusion | flops 25785532416 | bytes 61900800 | tf_op jit(solution)/shard_map/td,kdc->ktc/dot_general | solution.py:43
  171.3 0.7 slice.104
  172.0 2.1 collective-permute-start
  175.2 41.1 %tile.4 = f32[1024,128,256]{2,1,0:T(8,128)} broadcast(f32[1024,256]{1,0:T(8,128)S(1)} %pad_maximum_fusion), dimensions={0,2} | broadcast | bytes 135266304 | tf_op jit(solution)/shard_map/tile | solution.py:67
  216.3 108.6 %copy.69 = f32[128,8,128,256]{3,1,2,0:T(8,128)} copy(f32[128,8,128,256]{3,2,1,0:T(8,128)} %bitcast.28) | data formatting | bytes 268435456
  324.9 87.6 %slice.117 = f32[1024,32640]{1,0:T(8,128)} slice(f32[1024,32768]{1,0:T(8,128)} %bitcast.29), slice={[0:1024], [0:32640]} | slice | bytes 267386880 | tf_op jit(solution)/shard_map/slice | solution.py:67
  412.5 211.3 %reshape.29 = f32[1024,128,255]{2,1,0:T(8,128)} reshape(f32[1024,32640]{1,0:T(8,128)} %slice.117) | data formatting | bytes 267386880 | tf_op jit(solution)/shard_map/reshape | solution.py:68
  623.8 4.4 maximum_convert_fusion
  628.3 19.9 %fusion.11 = f32[3,512,1024]{2,1,0:T(8,128)} fusion(f32[3,518,1024]{2,1,0:T(8,128)} %maximum_convert_fusion, f32[3,1024]{1,0:T(4,128)S(1)} %copy-done.11, f32[3,1024]{1,0:T(4,128)S(1)} %copy-done.12, f32[3,1024]{1,0:T(4,128)S(1)} %copy-done.13, f32[3,1024]{1,0:T(4,128)S(1)} %copy-done.14, f32[3,1024]{1,0:T(4,128)S(1)} %copy-done.15, ...), kind=kLoop, calls=%fused_computation.15 | loop fusion | flops 20447232 | bytes 50417664 | tf_op jit(solution)/shard_map/add | solution.py:51
  648.1 4.1 slice_multiply_fusion.7
  652.2 2.0 copy.57
  654.3 110.2 %fusion = f32[1024,4,128]{2,1,0:T(4,128)} fusion(f32[4,128,1024]{1,0,2:T(4,128)S(1)} %copy.57, f32[1024,128,255]{2,1,0:T(8,128)} %reshape.29), kind=kOutput, calls=%fused_computation.2 | convolution fusion | flops 805306368 | bytes 71303168 | tf_op jit(solution)/shard_map/cts,ksc->ktc/dot_general | solution.py:70
  764.5 14.8 %fusion.5 = f32[1024,16,4]{1,2,0:T(4,128)} fusion(f32[4,128,1024]{1,0,2:T(4,128)S(1)} %copy.57, f32[128]{0:T(128)S(1)} %copy-done.21, f32[16,1024]{0,1:T(8,128)S(1)} %copy-done.9), kind=kOutput, calls=%fused_computation.7 | convolution fusion | flops 102760448 | bytes 2425344 | tf_op jit(solution)/shard_map/ksc,snc->knc/dot_general | solution.py:74
  779.4 2.0 copy.59
  781.4 0.7 fusion.29
  782.0 1.9 all-gather
  783.9 1.9 all-gather.1
  785.8 1.0 maximum_add_fusion
  786.9 1.9 copy.60
  788.7 12.9 %add_bitcast_fusion = f32[4,128,1024]{1,0,2:T(4,128)} fusion(f32[1024,4,128]{2,1,0:T(4,128)S(1)} %copy-done.2, f32[4,16,1024]{1,0,2:T(4,128)} %copy.60, f32[16,1024]{0,1:T(8,128)S(1)} %copy-done.7, f32[16,1024]{0,1:T(8,128)S(1)} %copy-done.9), kind=kOutput, calls=%fused_computation.44 | convolution fusion | flops 105381888 | bytes 4587520 | tf_op jit(solution)/shard_map/tnc,knc->ktc/dot_general | solution.py:93
  801.6 1.9 copy.61
  803.6 3.7 fusion.25
  807.3 15.6 %fusion.37 = f32[512,8192]{1,0:T(8,128)} fusion(bf16[512,1024]{1,0:T(8,128)(2,1)S(1)} %fusion.25, bf16[1024,8192]{1,0:T(8,128)(2,1)} %param.17), kind=kOutput, calls=%fused_computation.71 | convolution fusion | flops 8589934592 | bytes 34603008 | tf_op jit(solution)/shard_map/dot_general | solution.py:96
  822.9 281.6 %reduce-scatter.2.cloned.1.call-done = f32[512,1024]{1,0:T(8,128)} async-done(((f32[512,8192]{1,0:T(8,128)}), f32[512,1024]{1,0:T(8,128)}) %reduce-scatter.2.cloned.1.call-update) | async-done | bytes 2097168 | tf_op jit(solution)/shard_map/reduce_scatter | solution.py:97
  1104.5 2.9 fusion.23
  (64 shorter events, 4.4 us)
Async XLA Ops:
  6.5 15.7 %copy-start = (bf16[512,1024]{1,0:T(8,128)(2,1)S(1)}, bf16[512,1024]{1,0:T(8,128)(2,1)}, u32[]{:S(2)}) copy-start(bf16[512,1024]{1,0:T(8,128)(2,1)} %param.10) | copy-start | bytes 3145732
  6.5 40.3 %copy-start.10 = (f32[3,7,1024]{2,1,0:T(8,128)S(1)}, f32[3,7,1024]{2,1,0:T(8,128)}, u32[]{:S(2)}) copy-start(f32[3,7,1024]{2,1,0:T(8,128)} %param.13) | copy-start | bytes 258052
  6.5 131.0 %copy-start.20 = (f32[8192]{0:T(1024)S(1)}, f32[8192]{0:T(1024)}, u32[]{:S(2)}) copy-start(f32[8192]{0:T(1024)} %param.11) | copy-start | bytes 98308
  6.5 131.0 %all-gather.4.cloned.1.call-start = ((), (), s32[]{:S(2)}) async-start(), calls=%async_computation.1 | async-start | bytes 9437184 | tf_op jit(solution)/shard_map/all_gather | solution.py:41
  7.3 1097.3 %reduce-scatter.2.cloned.1.call-start = ((), (), s32[]{:S(2)}) async-start(), calls=%async_computation.2 | async-start | bytes 18874368 | tf_op jit(solution)/shard_map/reduce_scatter | solution.py:97
  8.3 12.9 %copy-start.6 = (f32[16,1024]{0,1:T(8,128)}, f32[16,1024]{0,1:T(8,128)S(1)}, u32[]{:S(2)}) copy-start(f32[16,1024]{0,1:T(8,128)S(1)} %copy.56) | copy-start | bytes 196612
  9.4 11.8 %copy-start.8 = (f32[16,1024]{0,1:T(8,128)}, f32[16,1024]{0,1:T(8,128)S(1)}, u32[]{:S(2)}) copy-start(f32[16,1024]{0,1:T(8,128)S(1)} %copy.55) | copy-start | bytes 196612
  171.3 45.0 %copy-start.3 = (bf16[3,512,1024]{2,1,0:T(8,128)(2,1)}, bf16[3,512,1024]{2,1,0:T(8,128)(2,1)S(1)}, u32[]{:S(2)}) copy-start(bf16[3,512,1024]{2,1,0:T(8,128)(2,1)S(1)} %fusion.21) | copy-start | bytes 9437188
  172.0 451.8 %collective-permute-start = (bf16[3,6,1024]{2,1,0:T(8,128)(2,1)}, bf16[3,6,1024]{2,1,0:T(8,128)(2,1)}, u32[]{:S(2)}, u32[]{:S(2)}) collective-permute-start(bf16[3,6,1024]{2,1,0:T(8,128)(2,1)} %slice.104), channel_id=1, source_target_pairs={{0,1},{2,3},{4,5},{6,7},{8,9},{10,11},{12,13},{14,15},{16,17},{18,... | collective-permute-start | bytes 110600 | tf_op jit(solution)/shard_map/ppermute | solution.py:12
  412.5 211.3 %copy-start.4 = (bf16[3,512,1024]{2,1,0:T(8,128)(2,1)S(1)}, bf16[3,512,1024]{2,1,0:T(8,128)(2,1)}, u32[]{:S(2)}) copy-start(bf16[3,512,1024]{2,1,0:T(8,128)(2,1)} %copy-done.3) | copy-start | bytes 9437188
  623.7 4.5 copy-start.11
  623.7 4.5 copy-start.12
  623.7 4.5 copy-start.13
  623.7 4.5 copy-start.14
  623.7 4.5 copy-start.15
  623.7 4.5 copy-start.16
  623.7 4.5 copy-start.17
  654.3 110.2 %copy-start.9 = (f32[16,1024]{0,1:T(8,128)S(1)}, f32[16,1024]{0,1:T(8,128)}, u32[]{:S(2)}) copy-start(f32[16,1024]{0,1:T(8,128)} %copy-done.8) | copy-start | bytes 196612
  654.3 110.2 %copy-start.21 = (f32[128]{0:T(128)S(1)}, f32[128]{0:T(128)}, u32[]{:S(2)}) copy-start(f32[128]{0:T(128)} %iota_subtract_fusion) | copy-start | bytes 1540
  764.5 16.9 %copy-start.5 = (f32[16,1024]{1,0:T(8,128)S(1)}, f32[16,1024]{1,0:T(8,128)}, u32[]{:S(2)}) copy-start(f32[16,1024]{1,0:T(8,128)} %param.14) | copy-start | bytes 196612
  764.5 21.3 %copy-start.19 = (f32[4]{0:T(128)S(1)}, f32[4]{0:T(128)}, u32[]{:S(2)}) copy-start(f32[4]{0:T(128)} %iota_multiply_fusion) | copy-start | bytes 52
  764.5 24.2 %copy-start.7 = (f32[16,1024]{0,1:T(8,128)S(1)}, f32[16,1024]{0,1:T(8,128)}, u32[]{:S(2)}) copy-start(f32[16,1024]{0,1:T(8,128)} %copy-done.6) | copy-start | bytes 196612
  779.4 9.4 copy-start.2
  788.7 14.8 %copy-start.18 = (f32[1024]{0:T(1024)S(1)}, f32[1024]{0:T(1024)}, u32[]{:S(2)}) copy-start(f32[1024]{0:T(1024)} %param.16) | copy-start | bytes 12292
  822.9 281.7 %copy-start.1 = (bf16[512,1024]{1,0:T(8,128)(2,1)S(1)}, bf16[512,1024]{1,0:T(8,128)(2,1)}, u32[]{:S(2)}) copy-start(bf16[512,1024]{1,0:T(8,128)(2,1)} %param.10) | copy-start | bytes 3145732
Sparse Core Ops, SparseCore 0:
  9.5 127.9 all-gather.3
  823.0 281.4 reduce-scatter.1
where the time goes:
time: 1120 us; the launch traced here: 1110 us
  local copies, waits for them, and re-layouts  463 us (41%)
  waiting for transfers between devices  371 us (33%)
  matrix products  187 us (17%)
  other arithmetic  50 us (4%)
  blocking collectives  27.6 us (2%)
  between operations  13.9 us (1%)
    reduce_scatter x1, waiting for transfers between devices, per_device(): lax.psum_scatter(partial_sums, 'chan', scatter_dimension=1, tiled=True)  282 us
    reshape x1, local copies, waits for them, and re-layouts, per_device(): tiled.reshape(chan_width, blk_size, 2 * blk_size - 1)[:, :, :blk_size]  211 us
    unnamed x51, local copies, waits for them, and re-layouts  113 us
    dot_general x1, matrix products, per_device(): jnp.einsum('cts,ksc->ktc', toeplitz, product_blocks, precision=lax.Precis...  110 us
    all_gather x1, waiting for transfers between devices, per_device(): lax.all_gather(tokens, 'chan', axis=1, tiled=True).astype(jnp.float32)  88.5 us
    slice x1, local copies, waits for them, and re-layouts, per_device(): jnp.tile(padded_filt, (1, blk_size))[:, :blk_size * (2 * blk_size - 1)]  87.6 us
    another operation x1, local copies, waits for them, and re-layouts, per_device(): jnp.tile(padded_filt, (1, blk_size))[:, :blk_size * (2 * blk_size - 1)]  41.1 us
    dot_general x1, matrix products, per_device(): jnp.einsum('td,kdc->ktc', scaled, in_weight, preferred_element_type=jnp.f...  33.8 us
  transfers between devices with their start and end apart: 3, of which 2 were waited for; matrix products, arithmetic and copies ran while one was open for 42% of the time, Pallas kernels for 0%

commit v1 on v0

v1 whole, which is shorter than its diff:
```python
import functools

import jax
import jax.numpy as jnp
from jax import lax
from jax.experimental import pallas as pl
from jax.experimental.pallas import tpu as pltpu
from jax.sharding import PartitionSpec as P

EPSILON = 1e-06
LANES = 128
MIB = 1024 * 1024


def from_behind(block, axis, distance):
    count = lax.axis_size(axis)
    route = [(i - distance, i) for i in range(count) if i - distance >= 0]
    return lax.ppermute(block, axis, route)


def proj_kernel(width, x_ref, gain_ref, w_ref, out_ref, scaled_ref, acc_ref, sq_ref):
    feat, step = pl.program_id(0), pl.program_id(1)
    depth = x_ref.shape[1]
    here = pl.ds(pl.multiple_of(step * depth, depth), depth)

    @pl.when(feat == 0)
    def _():
        x = x_ref[...].astype(jnp.float32)
        part = jnp.sum(x * x, axis=1, keepdims=True)

        @pl.when(step == 0)
        def _():
            sq_ref[...] = part

        @pl.when(step > 0)
        def _():
            sq_ref[...] += part

        scaled_ref[:, here] = (x * gain_ref[...]).astype(jnp.bfloat16)

    part = jnp.dot(scaled_ref[:, here], w_ref[0], preferred_element_type=jnp.float32)

    @pl.when(step == 0)
    def _():
        acc_ref[...] = part

    @pl.when(step > 0)
    def _():
        acc_ref[...] += part

    @pl.when(step == pl.num_programs(1) - 1)
    def _():
        inv_rms = lax.rsqrt(sq_ref[...] / width + EPSILON)
        for g in range(out_ref.shape[2]):
            cols = acc_ref[:, g * LANES : (g + 1) * LANES] * inv_rms
            out_ref[0, :, g, :] = cols.astype(jnp.bfloat16).astype(jnp.float32)


def project(tokens, gain, in_weight):
    rows, width = tokens.shape
    chans = in_weight.shape[2]
    depth = min(1024, width)
    groups = chans // LANES
    steps = width // depth
    return pl.pallas_call(
        functools.partial(proj_kernel, width),
        grid=(3, steps),
        in_specs=[
            pl.BlockSpec((rows, depth), lambda i, k: (0, jnp.where(i == 0, k, steps - 1))),
            pl.BlockSpec((1, depth), lambda i, k: (0, jnp.where(i == 0, k, steps - 1))),
            pl.BlockSpec((1, depth, chans), lambda i, k: (i, k, 0)),
        ],
        out_specs=pl.BlockSpec((1, rows, groups, LANES), lambda i, k: (i, 0, 0, 0)),
        out_shape=jax.ShapeDtypeStruct((3, rows, groups, LANES), jnp.float32),
        scratch_shapes=[
            pltpu.VMEM((rows, width), jnp.bfloat16),
            pltpu.VMEM((rows, chans), jnp.float32),
            pltpu.VMEM((rows, 1), jnp.float32),
        ],
        compiler_params=pltpu.CompilerParams(vmem_limit_bytes=48 * MIB),
        cost_estimate=pl.CostEstimate(
            flops=2 * rows * width * 3 * chans,
            bytes_accessed=2 * 3 * width * chans + 2 * rows * width + 12 * rows * chans,
            transcendentals=0,
        ),
        name="project",
    )(tokens, gain[None, :], in_weight)


def tree_sum(terms):
    while len(terms) > 1:
        pairs = [terms[i] + terms[i + 1] for i in range(0, len(terms) - 1, 2)]
        terms = pairs + terms[len(pairs) * 2 :]
    return terms[0]


def mix_kernel(proj_ref, rim_ref, taps_ref, decay_ref, res_ref, skip_ref, q_ref, base_ref, end_ref, win_ref, state_ref):
    step = pl.program_id(0)
    rows = proj_ref.shape[1]
    tap_count = taps_ref.shape[1]
    poles = decay_ref.shape[0]
    keep = rim_ref.shape[1]

    @pl.when(step == 0)
    def _():
        win_ref[:, :keep] = rim_ref[...]
        state_ref[...] = jnp.zeros_like(state_ref)

    win_ref[:, keep:] = proj_ref[...]
    decay = [jnp.exp(decay_ref[n]) for n in range(poles)]
    unroll = 8

    def body(blk, state):
        state = list(state)
        first = blk * unroll
        conv = []
        for i in range(3):
            taps = [taps_ref[i, j] for j in range(tap_count)]
            held = [win_ref[i, first + keep - (tap_count - 1) + r] for r in range(unroll + tap_count - 1)]
            conv.append(
                [
                    functools.reduce(
                        lambda a, b: a + b, [taps[j] * held[r + tap_count - 1 - j] for j in range(tap_count)]
                    )
                    for r in range(unroll)
                ]
            )
        for r in range(unroll):
            query, product = conv[0][r], conv[1][r] * conv[2][r]
            terms = [skip_ref[0] * product]
            for n in range(poles):
                state[n] = decay[n] * state[n] + product
                terms.append(res_ref[n] * state[n])
            q_ref[first + r] = query
            base_ref[first + r] = query * tree_sum(terms)
        return tuple(state)

    state = lax.fori_loop(0, rows // unroll, body, tuple(state_ref[n] for n in range(poles)))
    for n in range(poles):
        state_ref[n] = state[n]
    win_ref[:, :keep] = win_ref[:, rows:]

    @pl.when(step == pl.num_programs(0) - 1)
    def _():
        for n in range(poles):
            end_ref[n] = state[n]


def mix(proj, rim, taps, log_decay, residue, skip):
    rows, groups = proj.shape[1:3]
    tap_count, poles = taps.shape[1], log_decay.shape[0]
    keep = rim.shape[1]
    blk = min(128, rows)
    whole = lambda *shape: pl.BlockSpec(shape, lambda t: (0,) * len(shape))
    row_spec = pl.BlockSpec((blk, groups, LANES), lambda t: (t, 0, 0))
    return pl.pallas_call(
        mix_kernel,
        grid=(rows // blk,),
        in_specs=[
            pl.BlockSpec((3, blk, groups, LANES), lambda t: (0, t, 0, 0)),
            whole(3, keep, groups, LANES),
            whole(3, tap_count, groups, LANES),
            whole(poles, groups, LANES),
            whole(poles, groups, LANES),
            whole(1, groups, LANES),
        ],
        out_specs=[row_spec, row_spec, whole(poles, groups, LANES)],
        out_shape=[
            jax.ShapeDtypeStruct((rows, groups, LANES), jnp.float32),
            jax.ShapeDtypeStruct((rows, groups, LANES), jnp.float32),
            jax.ShapeDtypeStruct((poles, groups, LANES), jnp.float32),
        ],
        scratch_shapes=[
            pltpu.VMEM((3, keep + blk, groups, LANES), jnp.float32),
            pltpu.VMEM((poles, groups, LANES), jnp.float32),
        ],
        compiler_params=pltpu.CompilerParams(vmem_limit_bytes=48 * MIB),
        cost_estimate=pl.CostEstimate(
            flops=110 * rows * groups * LANES, bytes_accessed=20 * rows * groups * LANES, transcendentals=0
        ),
        name="mix",
    )(proj, rim, taps, log_decay, residue, skip)


def carry_kernel(q_ref, base_ref, state_ref, decay_ref, res_ref, out_ref, coef_ref, row_ref):
    step = pl.program_id(0)
    rows, groups = q_ref.shape[:2]
    poles = decay_ref.shape[0]
    decay = [jnp.exp(decay_ref[n]) for n in range(poles)]

    @pl.when(step == 0)
    def _():
        for n in range(poles):
            coef_ref[n] = res_ref[n] * (decay[n] * state_ref[n])

    unroll = 8

    def body(blk, coef):
        coef = list(coef)
        for r in range(unroll):
            t = blk * unroll + r
            row_ref[t] = base_ref[t] + q_ref[t] * tree_sum(list(coef))
            for n in range(poles):
                coef[n] = decay[n] * coef[n]
        return tuple(coef)

    coef = lax.fori_loop(0, rows // unroll, body, tuple(coef_ref[n] for n in range(poles)))
    for n in range(poles):
        coef_ref[n] = coef[n]
    for g in range(groups):
        out_ref[:, g * LANES : (g + 1) * LANES] = row_ref[:, g, :].astype(jnp.bfloat16)


def carry(query, base, state, log_decay, residue):
    rows, groups = query.shape[:2]
    poles = log_decay.shape[0]
    blk = min(128, rows)
    whole = lambda *shape: pl.BlockSpec(shape, lambda t: (0,) * len(shape))
    row_spec = pl.BlockSpec((blk, groups, LANES), lambda t: (t, 0, 0))
    return pl.pallas_call(
        carry_kernel,
        grid=(rows // blk,),
        in_specs=[row_spec, row_spec] + [whole(poles, groups, LANES)] * 3,
        out_specs=pl.BlockSpec((blk, groups * LANES), lambda t: (t, 0)),
        out_shape=jax.ShapeDtypeStruct((rows, groups * LANES), jnp.bfloat16),
        scratch_shapes=[
            pltpu.VMEM((poles, groups, LANES), jnp.float32),
            pltpu.VMEM((blk, groups, LANES), jnp.float32),
        ],
        compiler_params=pltpu.CompilerParams(vmem_limit_bytes=48 * MIB),
        cost_estimate=pl.CostEstimate(
            flops=40 * rows * groups * LANES, bytes_accessed=10 * rows * groups * LANES, transcendentals=0
        ),
        name="carry",
    )(query, base, state, log_decay, residue)


def per_device(tokens, norm_gain, in_weight, short_weight, log_decay, residue, skip, out_weight):
    rows, chans = tokens.shape
    groups = chans // LANES
    by_lane = lambda a: a.reshape(a.shape[:-1] + (groups, LANES))
    taps, log_decay, residue = by_lane(short_weight), by_lane(log_decay), by_lane(residue)
    skip = by_lane(skip[None, :])

    gathered = lax.all_gather(tokens, "chan", axis=1, tiled=True)
    proj = project(gathered, norm_gain, in_weight)
    rim = from_behind(proj[:, rows - 8 :], "seq", 1)
    query, base, end = mix(proj, rim, taps, log_decay, residue, skip)
    shard_decay = jnp.exp(rows * log_decay)
    state, passing = jnp.zeros_like(end), end
    for _ in range(lax.axis_size("seq") - 1):
        passing = from_behind(passing, "seq", 1)
        state = state + passing
        passing = passing * shard_decay
    gated = carry(query, base, state, log_decay, residue)
    partial = jnp.dot(gated, out_weight, preferred_element_type=jnp.float32)
    branch = lax.psum_scatter(partial.astype(jnp.bfloat16), "chan", scatter_dimension=1, tiled=True)
    return (tokens.astype(jnp.float32) + branch.astype(jnp.float32)).astype(jnp.bfloat16)


def solution(mesh):
    return jax.shard_map(
        per_device,
        mesh=mesh,
        in_specs=(
            P(("groups", "seq"), "chan"),
            P(),
            P(None, None, "chan"),
            P(None, None, "chan"),
            P(None, "chan"),
            P(None, "chan"),
            P("chan"),
            P("chan", None),
        ),
        out_specs=P(("groups", "seq"), "chan"),
        check_vma=False,
    )
```

time: 1120 us -> 385 us (0.34)
  local copies, waits for them, and re-layouts: 463 us -> 1.72 us
  matrix products: 187 us -> 16.8 us
  waiting for transfers between devices: 371 us -> 281 us
  Pallas kernels: 0 us -> 65.7 us
  other arithmetic: 50 us -> 2.59 us
  blocking collectives: 27.6 us -> 0 us
    reshape x1, local copies, waits for them, and re-layouts: 211 us -> 0.02 us  [per_device(): by_lane = lambda a: a.reshape(a.shape[:-1] + (groups, LANES))]
    dot_general x5 -> x1, matrix products: 187 us -> 16.8 us  [per_device(): partial = jnp.dot(gated, out_weight, preferred_element_type=jnp.float32)]
    reduce_scatter x1, waiting for transfers between devices: 282 us -> 148 us  [per_device(): lax.psum_scatter(partial.astype(jnp.bfloat16), 'chan', scatter_dimension=...]
    unnamed x51 -> x14, local copies, waits for them, and re-layouts: 113 us -> 0.81 us
    slice x4 -> x1, local copies, waits for them, and re-layouts: 88.5 us -> 0.9 us  [per_device(): rim = from_behind(proj[:, rows - 8:], 'seq', 1)]
    pallas_call x0 -> x3, Pallas kernels: none -> 65.7 us  [the longest x1 49.3 us: project(): pl.pallas_call(functools.partial(proj_kernel, width), grid=(3, steps), in...]
    all_gather x1, waiting for transfers between devices: 88.5 us -> 130 us  [per_device(): gathered = lax.all_gather(tokens, 'chan', axis=1, tiled=True)]
    another operation x3 -> x0, local copies, waits for them, and re-layouts: 41.1 us -> none  [the longest x1 41.1 us: per_device(): jnp.tile(padded_filt, (1, blk_size))[:, :blk_size * (2 * blk_size - 1)]]
  transfers between devices with their start and end apart: 3 -> 4, of which waited for: 2 -> 4; matrix products, arithmetic and copies ran while one was open for 42% -> 0% of each run, Pallas kernels for 0% -> 0%
where the time goes in v1:
time: 385 us
  waiting for transfers between devices  281 us (73%)
  Pallas kernels  65.7 us (17%)
  matrix products  16.8 us (4%)
  between operations  13.5 us (4%)
    reduce_scatter x1, waiting for transfers between devices, per_device(): lax.psum_scatter(partial.astype(jnp.bfloat16), 'chan', scatter_dimension=...  148 us
    all_gather x1, waiting for transfers between devices, per_device(): gathered = lax.all_gather(tokens, 'chan', axis=1, tiled=True)  130 us
    pallas_call x1, Pallas kernels, project(): pl.pallas_call(functools.partial(proj_kernel, width), grid=(3, steps), in...  49.3 us
    dot_general x1, matrix products, per_device(): partial = jnp.dot(gated, out_weight, preferred_element_type=jnp.float32)  16.8 us
    pallas_call x1, Pallas kernels, mix(): pl.pallas_call(mix_kernel, grid=(rows // blk,), in_specs=[pl.BlockSpec((3...  11.7 us
  transfers between devices with their start and end apart: 4, of which 4 were waited for; matrix products, arithmetic and copies ran while one was open for 0% of the time, Pallas kernels for 0%

profile of v1, /device:TPU:0, one launch (start us, length us, event | category | flops | bytes accessed | tf_op | source)
XLA Modules:
  0.0 384.6 jit_solution(8794785725132059373)
XLA Ops:
  6.5 0.0 all-gather.2.cloned.1.call-start
  6.5 0.7 all-gather.2.cloned.1.call-update
  7.3 0.0 reduce-scatter.2.cloned.1.call-start
  7.3 129.9 %all-gather.2.cloned.1.call-done.x_ref = bf16[512,8192]{1,0:T(8,128)(2,1)} async-done(((bf16[512,1024]{1,0:T(8,128)(2,1)}), bf16[512,8192]{1,0:T(8,128)(2,1)}) %all-gather.2.cloned.1.call-update) | async-done | bytes 8388624 | tf_op jit(solution)/shard_map/all_gather | solution.py:245
  137.2 0.0 copy-start.1
  137.2 0.8 copy-done.1
  137.9 0.0 copy-start.4
  138.0 0.0 copy-start.5
  138.0 0.0 copy-start.3
  138.0 0.0 copy-start
  138.0 49.3 %project.1.proj_ref = f32[3,512,8,128]{3,2,1,0:T(8,128)} custom-call(bf16[512,8192]{1,0:T(8,128)(2,1)} %all-gather.2.cloned.1.call-done.x_ref, f32[1,8192]{1,0:T(1,128)S(1)} %bitcast.13, bf16[3,8192,1024]{2,1,0:T(8,128)(2,1)} %w_ref.1), custom_call_target="tpu_custom_call" | custom-call | flops 25769803776 | bytes 65011712 | tf_op jit(solution)/shard_map/project/pallas_call | solution.py:65
  187.3 0.9 slice.4
  188.2 1.3 collective-permute-start
  189.5 0.0 copy-done.4
  189.5 0.0 copy-done.5
  189.6 0.0 copy-done.3
  189.6 0.8 collective-permute-done.rim_ref
  190.4 0.0 copy-done
  190.4 11.7 %mix.1 = (f32[512,8,128]{2,1,0:T(8,128)S(1)}, f32[512,8,128]{2,1,0:T(8,128)S(1)}, f32[16,8,128]{2,1,0:T(8,128)S(1)}) custom-call(f32[3,512,8,128]{3,2,1,0:T(8,128)} %project.1.proj_ref, f32[3,8,8,128]{3,2,1,0:T(8,128)S(1)} %collective-permute-done.rim_ref, f32[3,7,8,128]{3,2,1,0:T(8,128)S(1)} %reshape.9.taps_ref, f32[16,8,128]{2,1,0:T(8,128)S(1)} %bitcast.8, ...), custom_call_target="tpu_custom_call" | custom-call | flops 57671680 | bytes 10485760 | tf_op jit(solution)/shard_map/mix/pallas_call | solution.py:156
  202.2 2.3 collective-permute-start.1
  204.4 0.9 collective-permute-done.1.state_ref
  205.3 4.7 %carry.1 = bf16[512,1024]{1,0:T(8,128)(2,1)S(1)} custom-call(f32[512,8,128]{2,1,0:T(8,128)S(1)} %get-tuple-element.8.q_ref, f32[512,8,128]{2,1,0:T(8,128)S(1)} %get-tuple-element.9.base_ref, f32[16,8,128]{2,1,0:T(8,128)S(1)} %collective-permute-done.1.state_ref, f32[16,8,128]{2,1,0:T(8,128)S(1)} %bitcast.9, f32[16,8,128]{2,1,0:T(8,128)S(1)} %bitcast.11), custom_call_target="tpu_custom_call" | custom-call | flops 20971520 | bytes 5242880 | tf_op jit(solution)/shard_map/carry/pallas_call | solution.py:220
  210.0 16.8 %convolution_convert_fusion = bf16[512,8192]{1,0:T(8,128)(2,1)} fusion(bf16[512,1024]{1,0:T(8,128)(2,1)S(1)} %carry.1, bf16[1024,8192]{1,0:T(8,128)(2,1)} %param.15), kind=kOutput, calls=%fused_computation | convolution fusion | flops 8594128896 | bytes 26214400 | tf_op jit(solution)/shard_map/dot_general | solution.py:256
  226.8 0.0 copy-start.2
  226.8 0.0 reduce-scatter.2.cloned.1.call-update
  226.8 148.3 %reduce-scatter.2.cloned.1.call-done = bf16[512,1024]{1,0:T(8,128)(2,1)} async-done(((bf16[512,8192]{1,0:T(8,128)(2,1)}), bf16[512,1024]{1,0:T(8,128)(2,1)}) %reduce-scatter.2.cloned.1.call-update) | async-done | bytes 1048592 | tf_op jit(solution)/shard_map/reduce_scatter | solution.py:257
  375.1 0.0 copy-done.2
  375.1 2.6 add_convert_fusion
  (3 shorter events, 0.0 us)
Async XLA Ops:
  6.5 130.7 %all-gather.2.cloned.1.call-start = ((), (), s32[]{:S(2)}) async-start(), calls=%async_computation.1 | async-start | bytes 9437184 | tf_op jit(solution)/shard_map/all_gather | solution.py:245
  7.3 367.9 %reduce-scatter.2.cloned.1.call-start = ((), (), s32[]{:S(2)}) async-start(), calls=%async_computation.2 | async-start | bytes 9437184 | tf_op jit(solution)/shard_map/reduce_scatter | solution.py:257
  137.2 0.8 copy-start.1
  137.9 51.6 %copy-start.4 = (f32[16,1024]{1,0:T(8,128)S(1)}, f32[16,1024]{1,0:T(8,128)}, u32[]{:S(2)}) copy-start(f32[16,1024]{1,0:T(8,128)} %param.12) | copy-start | bytes 196612
  138.0 51.6 %copy-start.5 = (f32[16,1024]{1,0:T(8,128)S(1)}, f32[16,1024]{1,0:T(8,128)}, u32[]{:S(2)}) copy-start(f32[16,1024]{1,0:T(8,128)} %param.13) | copy-start | bytes 196612
  138.0 51.6 %copy-start.3 = (f32[3,7,1024]{2,1,0:T(8,128)S(1)}, f32[3,7,1024]{2,1,0:T(8,128)}, u32[]{:S(2)}) copy-start(f32[3,7,1024]{2,1,0:T(8,128)} %param.11) | copy-start | bytes 258052
  138.0 52.5 %copy-start = (f32[1024]{0:T(1024)S(1)}, f32[1024]{0:T(1024)}, u32[]{:S(2)}) copy-start(f32[1024]{0:T(1024)} %param.14) | copy-start | bytes 12292
  188.2 2.3 collective-permute-start
  202.2 3.2 collective-permute-start.1
  226.8 148.4 %copy-start.2 = (bf16[512,1024]{1,0:T(8,128)(2,1)S(1)}, bf16[512,1024]{1,0:T(8,128)(2,1)}, u32[]{:S(2)}) copy-start(bf16[512,1024]{1,0:T(8,128)(2,1)} %param.8) | copy-start | bytes 3145732
Sparse Core Ops, SparseCore 0:
  9.5 127.6 all-gather.1
  226.9 148.1 reduce-scatter.1

commit v2 on v1

--- a/solution.py
+++ b/solution.py
@@ -92,6 +92,202 @@
         pairs = [terms[i] + terms[i + 1] for i in range(0, len(terms) - 1, 2)]
         terms = pairs + terms[len(pairs) * 2 :]
     return terms[0]
+
+
+def accumulate_kernel(count, width, first, last, place_ref, *refs):
+    chunk_refs, refs = refs[:count], refs[count:]
+    gain_ref, w_ref, refs = refs[0], refs[1], refs[2:]
+    if not first:
+        held_ref, held_sq_ref, refs = refs[0], refs[1], refs[2:]
+    if last:
+        out_ref, scaled_ref, acc_ref, sq_ref = refs
+    else:
+        acc_ref, sq_ref, scaled_ref = refs
+    feat, step = pl.program_id(0), pl.program_id(1)
+
+    for j in range(count):
+
+        @pl.when((feat == 0) & (step == j))
+        def _():
+            x = chunk_refs[j][...].astype(jnp.float32)
+            parts = [x[:, g : g + LANES] * x[:, g : g + LANES] for g in range(0, x.shape[1], LANES)]
+            part = tree_sum(parts)
+            if j > 0:
+                sq_ref[...] += part
+            elif first:
+                sq_ref[...] = part
+            else:
+                sq_ref[...] = held_sq_ref[...] + part
+            scaled_ref[j] = (x * gain_ref[0]).astype(jnp.bfloat16)
+
+    part = jnp.dot(scaled_ref[step], w_ref[0], preferred_element_type=jnp.float32)
+    acc = acc_ref if last else acc_ref.at[0]
+
+    @pl.when(step == 0)
+    def _():
+        acc[...] = part if first else held_ref[0] + part
+
+    if count > 1:
+
+        @pl.when(step > 0)
+        def _():
+            acc[...] += part
+
+    if last:
+
+        @pl.when(step == count - 1)
+        def _():
+            total = jnp.sum(sq_ref[...], axis=1, keepdims=True)
+            inv_rms = lax.rsqrt(total / width + EPSILON)
+            for g in range(out_ref.shape[2]):
+                cols = acc[:, g * LANES : (g + 1) * LANES] * inv_rms
+                out_ref[0, :, g, :] = cols.astype(jnp.bfloat16).astype(jnp.float32)
+
+
+def accumulate(chunks, places, gain, in_weight, held=None, last=False):
+    count, (rows, depth) = len(chunks), chunks[0].shape
+    width, chans = in_weight.shape[1:]
+    groups = chans // LANES
+    first = held is None
+    feat_spec = pl.BlockSpec((1, rows, chans), lambda i, k, p: (i, 0, 0))
+    sq_spec = pl.BlockSpec((rows, LANES), lambda i, k, p: (0, 0))
+    in_specs = [pl.BlockSpec((rows, depth), lambda i, k, p: (0, 0))] * count + [
+        pl.BlockSpec((1, 1, depth), lambda i, k, p: (p[jnp.where(i == 0, k, count - 1)], 0, 0)),
+        pl.BlockSpec((1, depth, chans), lambda i, k, p: (i, p[k], 0)),
+    ]
+    scratch = [pltpu.VMEM((count, rows, depth), jnp.bfloat16)]
+    if last:
+        out_specs = pl.BlockSpec((1, rows, groups, LANES), lambda i, k, p: (i, 0, 0, 0))
+        out_shape = jax.ShapeDtypeStruct((3, rows, groups, LANES), jnp.float32)
+        scratch += [pltpu.VMEM((rows, chans), jnp.float32), pltpu.VMEM((rows, LANES), jnp.float32)]
+    else:
+        out_specs = [feat_spec, sq_spec]
+        out_shape = [
+            jax.ShapeDtypeStruct((3, rows, chans), jnp.float32),
+            jax.ShapeDtypeStruct((rows, LANES), jnp.float32),
+        ]
+    extra, aliases = (), {}
+    if not first:
+        in_specs += [feat_spec, sq_spec]
+        extra = tuple(held)
+        if not last:
+            aliases = {count + 3: 0, count + 4: 1}
+    return pl.pallas_call(
+        functools.partial(accumulate_kernel, count, width, first, last),
+        grid_spec=pltpu.PrefetchScalarGridSpec(
+            num_scalar_prefetch=1,
+            grid=(3, count),
+            in_specs=in_specs,
+            out_specs=out_specs,
+            scratch_shapes=scratch,
+        ),
+        out_shape=out_shape,
+        input_output_aliases=aliases,
+        compiler_params=pltpu.CompilerParams(vmem_limit_bytes=48 * MIB),
+        cost_estimate=pl.CostEstimate(
+            flops=2 * rows * depth * count * 3 * chans,
+            bytes_accessed=6 * depth * count * chans + 24 * rows * chans,
+            transcendentals=0,
+        ),
+        name="accumulate",
+    )(jnp.stack(places).astype(jnp.int32), *chunks, gain.reshape(-1, 1, depth), in_weight, *extra)
+
+
+def piece_kernel(place_ref, gated_ref, w_ref, *refs):
+    total = jnp.dot(gated_ref[...], w_ref[...], preferred_element_type=jnp.float32)
+    for ref in refs[:-1]:
+        total = total + ref[...].astype(jnp.float32)
+    refs[-1][...] = total.astype(jnp.bfloat16)
+
+
+def piece(gated, out_weight, place, *terms):
+    rows, chans = gated.shape
+    tile = min(512, chans)
+    tiles = chans // tile
+    spec = pl.BlockSpec((rows, tile), lambda t, p: (0, t))
+    return pl.pallas_call(
+        piece_kernel,
+        grid_spec=pltpu.PrefetchScalarGridSpec(
+            num_scalar_prefetch=1,
+            grid=(tiles,),
+            in_specs=[
+                pl.BlockSpec((rows, chans), lambda t, p: (0, 0)),
+                pl.BlockSpec((chans, tile), lambda t, p: (0, p[0] * tiles + t)),
+            ]
+            + [spec] * len(terms),
+            out_specs=spec,
+        ),
+        out_shape=jax.ShapeDtypeStruct((rows, chans), jnp.bfloat16),
+        compiler_params=pltpu.CompilerParams(vmem_limit_bytes=48 * MIB),
+        cost_estimate=pl.CostEstimate(
+            flops=2 * rows * chans * chans,
+            bytes_accessed=2 * chans * chans + 2 * rows * chans * (2 + len(terms)),
+            transcendentals=0,
+        ),
+        name="piece",
+    )(place.astype(jnp.int32)[None], gated, out_weight, *terms)
+
+
+def along_line(block, pairs):
+    return lax.ppermute(block, "chan", [(2 * a + y, 2 * b + y) for a, b in pairs for y in (0, 1)])
+
+
+def across(block):
+    count = lax.axis_size("chan")
+    return lax.ppermute(block, "chan", [(c, c ^ 1) for c in range(count)])
+
+
+def after(block, *earlier):
+    return lax.optimization_barrier((block,) + earlier)[0]
+
+
+PAIRS = [(0, 1), (1, 0), (2, 3), (3, 2)]
+MIDDLE = [(1, 2), (2, 1)]
+OUTWARD = [(1, 0), (2, 3)]
+INWARD = [(0, 1), (3, 2)]
+
+
+def gather_and_project(tokens, gain, in_weight):
+    me = lax.axis_index("chan")
+    mine = lambda k: me ^ (2 * k)
+    other = lambda k: me ^ (2 * k + 1)
+    at_end = (me < 2) | (me >= 6)
+    next_one = along_line(tokens, PAIRS)
+    middle = along_line(tokens, MIDDLE)
+    own_over = across(tokens)
+    held = accumulate([tokens], [me], gain, in_weight)
+    next_over = across(next_one)
+    second_out = along_line(middle, OUTWARD)
+    second_mid = along_line(next_one, MIDDLE)
+    held = accumulate([own_over, next_one], [other(0), mine(1)], gain, in_weight, held)
+    second = jnp.where(at_end, second_out, second_mid)
+    second_over = across(second)
+    third_out = along_line(second_mid, OUTWARD)
+    held = accumulate([next_over, second], [other(1), mine(2)], gain, in_weight, held)
+    third = jnp.where(at_end, third_out, middle)
+    third_over = across(third)
+    held = accumulate([second_over, third], [other(2), mine(3)], gain, in_weight, held)
+    return accumulate([third_over], [other(3)], gain, in_weight, held, last=True)
+
+
+def project_and_reduce(gated, out_weight, tokens):
+    me = lax.axis_index("chan")
+    at_mine = lambda k, *terms: piece(gated, out_weight, me ^ (2 * k), *terms)
+    at_other = lambda k: piece(gated, out_weight, me ^ (2 * k + 1))
+    third_over = across(at_other(3))
+    third = at_mine(3, third_over)
+    third_in = along_line(third, INWARD)
+    second_over = across(after(at_other(2), third_over))
+    second = at_mine(2, second_over, third_in)
+    second_in = along_line(second, INWARD)
+    second_mid = along_line(second, MIDDLE)
+    next_over = across(after(at_other(1), second_over))
+    next_one = at_mine(1, next_over, second_mid)
+    next_in = along_line(next_one, PAIRS)
+    middle = (third.astype(jnp.float32) + second_in.astype(jnp.float32)).astype(jnp.bfloat16)
+    middle_in = along_line(middle, MIDDLE)
+    own_over = across(after(at_other(0), next_over))
+    return at_mine(0, own_over, next_in, middle_in, tokens)
 
 
 def mix_kernel(proj_ref, rim_ref, taps_ref, decay_ref, res_ref, skip_ref, q_ref, base_ref, end_ref, win_ref, state_ref):
@@ -242,8 +438,12 @@
     taps, log_decay, residue = by_lane(short_weight), by_lane(log_decay), by_lane(residue)
     skip = by_lane(skip[None, :])
 
-    gathered = lax.all_gather(tokens, "chan", axis=1, tiled=True)
-    proj = project(gathered, norm_gain, in_weight)
+    paired_line = lax.axis_size("chan") == 8
+    if paired_line:
+        proj = gather_and_project(tokens, norm_gain, in_weight)
+    else:
+        gathered = lax.all_gather(tokens, "chan", axis=1, tiled=True)
+        proj = project(gathered, norm_gain, in_weight)
     rim = from_behind(proj[:, rows - 8 :], "seq", 1)
     query, base, end = mix(proj, rim, taps, log_decay, residue, skip)
     shard_decay = jnp.exp(rows * log_decay)
@@ -253,6 +453,8 @@
         state = state + passing
         passing = passing * shard_decay
     gated = carry(query, base, state, log_decay, residue)
+    if paired_line:
+        return project_and_reduce(gated, out_weight, tokens)
     partial = jnp.dot(gated, out_weight, preferred_element_type=jnp.float32)
     branch = lax.psum_scatter(partial.astype(jnp.bfloat16), "chan", scatter_dimension=1, tiled=True)
     return (tokens.astype(jnp.float32) + branch.astype(jnp.float32)).astype(jnp.bfloat16)

time: 385 us -> 281 us (0.73)
  waiting for transfers between devices: 281 us -> 132 us
  Pallas kernels: 65.7 us -> 107 us
  starting transfers between devices: 3.63 us -> 35.2 us
  matrix products: 16.8 us -> 0 us
  between operations: 13.5 us -> 0.25 us
    reduce_scatter x1 -> x0, waiting for transfers between devices: 148 us -> none  [per_device(): lax.psum_scatter(partial.astype(jnp.bfloat16), 'chan', scatter_dimension=...]
    ppermute x0 -> x18, waiting for transfers between devices: none -> 131 us  [the longest x10 91.3 us: along_line(): lax.ppermute(block, 'chan', [(2 * a + y, 2 * b + y) for a, b in pairs for...]
    all_gather x1 -> x0, waiting for transfers between devices: 130 us -> none  [per_device(): gathered = lax.all_gather(tokens, 'chan', axis=1, tiled=True)]
    pallas_call x1 -> x13, Pallas kernels: 49.3 us -> 90.2 us  [the longest x5 67.2 us: accumulate(): pl.pallas_call(functools.partial(accumulate_kernel, count, width, first,...]
    ppermute x0 -> x18, starting transfers between devices: none -> 31.4 us  [the longest x10 20.1 us: along_line(): lax.ppermute(block, 'chan', [(2 * a + y, 2 * b + y) for a, b in pairs for...]
    dot_general x1 -> x0, matrix products: 16.8 us -> none  [per_device(): partial = jnp.dot(gated, out_weight, preferred_element_type=jnp.float32)]
  transfers between devices with their start and end apart: 4 -> 20, of which waited for: 4 -> 14; matrix products, arithmetic and copies ran while one was open for 0% -> 1% of each run, Pallas kernels for 0% -> 24%
where the time goes in v2:
time: 281 us; the launch traced here: 280 us
  waiting for transfers between devices  132 us (47%)
  Pallas kernels  107 us (38%)
  starting transfers between devices  35.2 us (13%)
  other arithmetic  3.33 us (1%)
  local copies, waits for them, and re-layouts  2.95 us (1%)
    ppermute x10, waiting for transfers between devices, along_line(): lax.ppermute(block, 'chan', [(2 * a + y, 2 * b + y) for a, b in pairs for...  91.3 us
    pallas_call x5, Pallas kernels, accumulate(): pl.pallas_call(functools.partial(accumulate_kernel, count, width, first,...  67.2 us
    ppermute x8, waiting for transfers between devices, across(): return lax.ppermute(block, 'chan', [(c, c ^ 1) for c in range(count)])  39.2 us
    pallas_call x8, Pallas kernels, piece(): pl.pallas_call(piece_kernel, grid_spec=pltpu.PrefetchScalarGridSpec(num_s...  23.1 us
    ppermute x10, starting transfers between devices, along_line(): lax.ppermute(block, 'chan', [(2 * a + y, 2 * b + y) for a, b in pairs for...  20.1 us
    pallas_call x1, Pallas kernels, mix(): pl.pallas_call(mix_kernel, grid=(rows // blk,), in_specs=[pl.BlockSpec((3...  11.7 us
    ppermute x8, starting transfers between devices, across(): return lax.ppermute(block, 'chan', [(c, c ^ 1) for c in range(count)])  11.4 us
  transfers between devices with their start and end apart: 20, of which 14 were waited for; matrix products, arithmetic and copies ran while one was open for 1% of the time, Pallas kernels for 24%

profile of v2, /device:TPU:0, one launch (start us, length us, event | category | flops | bytes accessed | tf_op | source)
XLA Modules:
  0.0 280.3 jit_solution(14112475759534825567)
XLA Ops:
  0.0 3.0 %collective-permute-start = (bf16[512,1024]{1,0:T(8,128)(2,1)}, bf16[512,1024]{1,0:T(8,128)(2,1)S(1)}, u32[]{:S(2)}, u32[]{:S(2)}) collective-permute-start(bf16[512,1024]{1,0:T(8,128)(2,1)} %refs_3_.7), channel_id=1, source_target_pairs={{0,4},{2,6},{4,0},{6,2},{8,12},{10,14},{12,8},{14,10},{1,5},{3,7},... | collective-permute-start | bytes 3145736 | tf_op jit(solution)/shard_map/ppermute | solution.py:232
  3.7 22.6 %collective-permute-done.refs_1_ = bf16[512,1024]{1,0:T(8,128)(2,1)S(1)} collective-permute-done((bf16[512,1024]{1,0:T(8,128)(2,1)}, bf16[512,1024]{1,0:T(8,128)(2,1)S(1)}, u32[]{:S(2)}, u32[]{:S(2)}) %collective-permute-start) | collective-permute-done | bytes 1048608 | tf_op jit(solution)/shard_map/ppermute | solution.py:232
  29.3 1.8 collective-permute-start.8
  33.1 8.4 %accumulate.5 = (f32[3,512,1024]{2,1,0:T(8,128)}, f32[512,128]{1,0:T(8,128)S(1)}) custom-call(s32[1]{0:T(128)} %bitcast.place_ref, bf16[512,1024]{1,0:T(8,128)(2,1)S(1)} %copy-done, f32[8,1,1024]{2,1,0:T(1,128)S(1)} %bitcast.14, bf16[3,8192,1024]{2,1,0:T(8,128)(2,1)} %refs_2_.3), custom_call_target="tpu_custom_call" | custom-call | flops 3221225472 | bytes 18874368 | tf_op jit(solution)/shard_map/accumulate/pallas_call | solution.py:175
  43.3 12.0 %collective-permute-done.5 = bf16[512,1024]{1,0:T(8,128)(2,1)} collective-permute-done((bf16[512,1024]{1,0:T(8,128)(2,1)S(1)}, bf16[512,1024]{1,0:T(8,128)(2,1)}, u32[]{:S(2)}, u32[]{:S(2)}) %collective-permute-start.5) | collective-permute-done | bytes 1048608 | tf_op jit(solution)/shard_map/ppermute | solution.py:232
  58.3 15.7 %accumulate.6 = (f32[3,512,1024]{2,1,0:T(8,128)}, f32[512,128]{1,0:T(8,128)S(1)}) custom-call(s32[2]{0:T(128)S(1)} %pad_add_fusion.2.place_ref, bf16[512,1024]{1,0:T(8,128)(2,1)S(1)} %collective-permute-done.8.refs_0_, bf16[512,1024]{1,0:T(8,128)(2,1)S(1)} %collective-permute-done.refs_1_, ...), custom_call_target="tpu_custom_call", output_to_operand_aliasing={{0}: (5, {}), {1}: (6, {})} | custom-call | flops 6442450944 | bytes 25165824 | tf_op jit(solution)/shard_map/accumulate/pallas_call | solution.py:175
  73.9 3.5 %collective-permute-done.2 = bf16[512,1024]{1,0:T(8,128)(2,1)} collective-permute-done((bf16[512,1024]{1,0:T(8,128)(2,1)}, bf16[512,1024]{1,0:T(8,128)(2,1)}, u32[]{:S(2)}, u32[]{:S(2)}) %collective-permute-start.2) | collective-permute-done | bytes 1048608 | tf_op jit(solution)/shard_map/ppermute | solution.py:232
  80.4 15.7 %accumulate.7 = (f32[3,512,1024]{2,1,0:T(8,128)}, f32[512,128]{1,0:T(8,128)S(1)}) custom-call(s32[2]{0:T(128)S(1)} %pad_add_fusion.1.place_ref, bf16[512,1024]{1,0:T(8,128)(2,1)S(1)} %collective-permute-done.7.refs_0_, bf16[512,1024]{1,0:T(8,128)(2,1)S(1)} %broadcast_select_fusion.refs_1_, ...), custom_call_target="tpu_custom_call", output_to_operand_aliasing={{0}: (5, {}), {1}: (6, {})} | custom-call | flops 6442450944 | bytes 25165824 | tf_op jit(solution)/shard_map/accumulate/pallas_call | solution.py:175
  96.1 4.5 %collective-permute-done.6.refs_0_ = bf16[512,1024]{1,0:T(8,128)(2,1)S(1)} collective-permute-done((bf16[512,1024]{1,0:T(8,128)(2,1)S(1)}, bf16[512,1024]{1,0:T(8,128)(2,1)S(1)}, u32[]{:S(2)}, u32[]{:S(2)}) %collective-permute-start.6) | collective-permute-done | bytes 1048608 | tf_op jit(solution)/shard_map/ppermute | solution.py:237
  100.6 15.7 %accumulate.8 = (f32[3,512,1024]{2,1,0:T(8,128)}, f32[512,128]{1,0:T(8,128)S(1)}) custom-call(s32[2]{0:T(128)S(1)} %pad_add_fusion.place_ref, bf16[512,1024]{1,0:T(8,128)(2,1)S(1)} %collective-permute-done.6.refs_0_, bf16[512,1024]{1,0:T(8,128)(2,1)S(1)} %broadcast_select_fusion.1.refs_1_, ...), custom_call_target="tpu_custom_call", output_to_operand_aliasing={{0}: (5, {}), {1}: (6, {})} | custom-call | flops 6442450944 | bytes 25165824 | tf_op jit(solution)/shard_map/accumulate/pallas_call | solution.py:175
  116.3 5.0 %collective-permute-done.4.refs_0_ = bf16[512,1024]{1,0:T(8,128)(2,1)S(1)} collective-permute-done((bf16[512,1024]{1,0:T(8,128)(2,1)S(1)}, bf16[512,1024]{1,0:T(8,128)(2,1)S(1)}, u32[]{:S(2)}, u32[]{:S(2)}) %collective-permute-start.4) | collective-permute-done | bytes 1048608 | tf_op jit(solution)/shard_map/ppermute | solution.py:237
  121.3 11.8 %accumulate.9.proj_ref = f32[3,512,8,128]{3,2,1,0:T(8,128)} custom-call(s32[1]{0:T(128)} %bitcast.1.place_ref, bf16[512,1024]{1,0:T(8,128)(2,1)S(1)} %collective-permute-done.4.refs_0_, f32[8,1,1024]{2,1,0:T(1,128)S(1)} %bitcast.18, bf16[3,8192,1024]{2,1,0:T(8,128)(2,1)} %refs_2_.3, f32[3,512,1024]{2,1,0:T(8,128)} %get-tuple-element.25.refs_3_, ...), custom_call_target="tpu_custom_call" | custom-call | flops 3221225472 | bytes 18874368 | tf_op jit(solution)/shard_map/accumulate/pallas_call | solution.py:175
  136.2 11.7 %mix.1 = (f32[512,8,128]{2,1,0:T(8,128)S(1)}, f32[512,8,128]{2,1,0:T(8,128)S(1)}, f32[16,8,128]{2,1,0:T(8,128)S(1)}) custom-call(f32[3,512,8,128]{3,2,1,0:T(8,128)} %accumulate.9.proj_ref, f32[3,8,8,128]{3,2,1,0:T(8,128)S(1)} %collective-permute-done.9.rim_ref, f32[3,7,8,128]{3,2,1,0:T(8,128)S(1)} %reshape.17.taps_ref, f32[16,8,128]{2,1,0:T(8,128)S(1)} %bitcast.19, ...), custom_call_target="tpu_custom_call" | custom-call | flops 57671680 | bytes 10485760 | tf_op jit(solution)/shard_map/mix/pallas_call | solution.py:352
  148.0 2.4 collective-permute-start.10
  151.1 4.7 %carry.1.gated_ref = bf16[512,1024]{1,0:T(8,128)(2,1)S(1)} custom-call(f32[512,8,128]{2,1,0:T(8,128)S(1)} %get-tuple-element.27.q_ref, f32[512,8,128]{2,1,0:T(8,128)S(1)} %get-tuple-element.28.base_ref, f32[16,8,128]{2,1,0:T(8,128)S(1)} %collective-permute-done.10.state_ref, f32[16,8,128]{2,1,0:T(8,128)S(1)} %bitcast.20, f32[16,8,128]{2,1,0:T(8,128)S(1)} %bitcast.22), custom_call_target="tpu_custom_call" | custom-call | flops 20971520 | bytes 5242880 | tf_op jit(solution)/shard_map/carry/pallas_call | solution.py:416
  155.8 2.7 piece.11
  160.0 2.7 piece.10
  162.7 21.3 %collective-permute-done.11.refs_0_ = bf16[512,1024]{1,0:T(8,128)(2,1)S(1)} collective-permute-done((bf16[512,1024]{1,0:T(8,128)(2,1)S(1)}, bf16[512,1024]{1,0:T(8,128)(2,1)S(1)}, u32[]{:S(2)}, u32[]{:S(2)}) %collective-permute-start.11) | collective-permute-done | bytes 1048608 | tf_op jit(solution)/shard_map/ppermute | solution.py:237
  184.0 2.7 piece.12
  186.8 6.0 %collective-permute-start.15 = (bf16[512,1024]{1,0:T(8,128)(2,1)S(1)}, bf16[512,1024]{1,0:T(8,128)(2,1)S(1)}, u32[]{:S(2)}, u32[]{:S(2)}) collective-permute-start(bf16[512,1024]{1,0:T(8,128)(2,1)S(1)} %piece.12), channel_id=1, source_target_pairs={{0,4},{2,6},{12,8},{14,10},{1,5},{3,7},{13,9},{15,11},{16,20},{18,... | collective-permute-start | bytes 3145736 | tf_op jit(solution)/shard_map/ppermute | solution.py:232
  194.3 20.5 %collective-permute-done.15.refs_1_ = bf16[512,1024]{1,0:T(8,128)(2,1)S(1)} collective-permute-done((bf16[512,1024]{1,0:T(8,128)(2,1)S(1)}, bf16[512,1024]{1,0:T(8,128)(2,1)S(1)}, u32[]{:S(2)}, u32[]{:S(2)}) %collective-permute-start.15) | collective-permute-done | bytes 1048608 | tf_op jit(solution)/shard_map/ppermute | solution.py:232
  214.8 2.4 collective-permute-done.12.refs_0_
  217.2 2.8 %piece.13 = bf16[512,1024]{1,0:T(8,128)(2,1)S(1)} custom-call(s32[1]{0:T(128)} %bitcast.6.place_ref, bf16[512,1024]{1,0:T(8,128)(2,1)S(1)} %carry.1.gated_ref, bf16[1024,8192]{1,0:T(8,128)(2,1)} %w_ref.15, bf16[512,1024]{1,0:T(8,128)(2,1)S(1)} %collective-permute-done.12.refs_0_, bf16[512,1024]{1,0:T(8,128)(2,1)S(1)} %collective-permute-done.15.refs_1_), custom_call_target="tpu_custom_call" | custom-call | flops 1073741824 | bytes 6291456 | tf_op jit(solution)/shard_map/piece/pallas_call | solution.py:208
  220.0 2.1 collective-permute-start.18
  222.1 2.7 piece.9
  227.2 2.7 piece.8
  229.9 13.3 %collective-permute-done.18 = bf16[512,1024]{1,0:T(8,128)(2,1)S(1)} collective-permute-done((bf16[512,1024]{1,0:T(8,128)(2,1)S(1)}, bf16[512,1024]{1,0:T(8,128)(2,1)S(1)}, u32[]{:S(2)}, u32[]{:S(2)}) %collective-permute-start.18) | collective-permute-done | bytes 1048608 | tf_op jit(solution)/shard_map/ppermute | solution.py:232
  244.5 4.5 %collective-permute-done.13.refs_0_ = bf16[512,1024]{1,0:T(8,128)(2,1)S(1)} collective-permute-done((bf16[512,1024]{1,0:T(8,128)(2,1)S(1)}, bf16[512,1024]{1,0:T(8,128)(2,1)S(1)}, u32[]{:S(2)}, u32[]{:S(2)}) %collective-permute-start.13) | collective-permute-done | bytes 1048608 | tf_op jit(solution)/shard_map/ppermute | solution.py:237
  249.1 2.8 %piece.14 = bf16[512,1024]{1,0:T(8,128)(2,1)S(1)} custom-call(s32[1]{0:T(128)} %bitcast.8.place_ref, bf16[512,1024]{1,0:T(8,128)(2,1)S(1)} %carry.1.gated_ref, bf16[1024,8192]{1,0:T(8,128)(2,1)} %w_ref.15, bf16[512,1024]{1,0:T(8,128)(2,1)S(1)} %collective-permute-done.13.refs_0_, bf16[512,1024]{1,0:T(8,128)(2,1)S(1)} %collective-permute-done.16.refs_1_), custom_call_target="tpu_custom_call" | custom-call | flops 1073741824 | bytes 6291456 | tf_op jit(solution)/shard_map/piece/pallas_call | solution.py:208
  251.9 2.4 collective-permute-start.17
  255.9 19.2 %collective-permute-done.17.refs_1_ = bf16[512,1024]{1,0:T(8,128)(2,1)S(1)} collective-permute-done((bf16[512,1024]{1,0:T(8,128)(2,1)S(1)}, bf16[512,1024]{1,0:T(8,128)(2,1)S(1)}, u32[]{:S(2)}, u32[]{:S(2)}) %collective-permute-start.17) | collective-permute-done | bytes 1048608 | tf_op jit(solution)/shard_map/ppermute | solution.py:232
  276.6 3.8 %piece.15 = bf16[512,1024]{1,0:T(8,128)(2,1)} custom-call(s32[1]{0:T(128)} %bitcast.place_ref, bf16[512,1024]{1,0:T(8,128)(2,1)S(1)} %carry.1.gated_ref, bf16[1024,8192]{1,0:T(8,128)(2,1)} %w_ref.15, bf16[512,1024]{1,0:T(8,128)(2,1)S(1)} %collective-permute-done.14.refs_0_, bf16[512,1024]{1,0:T(8,128)(2,1)S(1)} %collective-permute-done.17.refs_1_, ...), custom_call_target="tpu_custom_call" | custom-call | flops 1073741824 | bytes 8388608 | tf_op jit(solution)/shard_map/piece/pallas_call | solution.py:208
  (49 shorter events, 26.7 us)
Async XLA Ops:
  0.0 26.4 %collective-permute-start = (bf16[512,1024]{1,0:T(8,128)(2,1)}, bf16[512,1024]{1,0:T(8,128)(2,1)S(1)}, u32[]{:S(2)}, u32[]{:S(2)}) collective-permute-start(bf16[512,1024]{1,0:T(8,128)(2,1)} %refs_3_.7), channel_id=1, source_target_pairs={{0,4},{2,6},{4,0},{6,2},{8,12},{10,14},{12,8},{14,10},{1,5},{3,7},... | collective-permute-start | bytes 3145736 | tf_op jit(solution)/shard_map/ppermute | solution.py:232
  3.0 25.0 %collective-permute-start.3 = (bf16[512,1024]{1,0:T(8,128)(2,1)}, bf16[512,1024]{1,0:T(8,128)(2,1)S(1)}, u32[]{:S(2)}, u32[]{:S(2)}) collective-permute-start(bf16[512,1024]{1,0:T(8,128)(2,1)} %refs_3_.7), channel_id=1, source_target_pairs={{4,8},{6,10},{8,4},{10,6},{5,9},{7,11},{9,5},{11,7},{20,24},{22,26... | collective-permute-start | bytes 3145736 | tf_op jit(solution)/shard_map/ppermute | solution.py:232
  26.4 15.1 %collective-permute-start.1 = (bf16[512,1024]{1,0:T(8,128)(2,1)S(1)}, bf16[512,1024]{1,0:T(8,128)(2,1)}, u32[]{:S(2)}, u32[]{:S(2)}) collective-permute-start(bf16[512,1024]{1,0:T(8,128)(2,1)S(1)} %collective-permute-done.refs_1_), channel_id=1, source_target_pairs={{4,8},{6,10},{8,4},{10,6},{5,9},{7,11},{9,5},{11,7},{20,24},{22,26... | collective-permute-start | bytes 3145736 | tf_op jit(solution)/shard_map/ppermute | solution.py:232
  28.0 27.3 %collective-permute-start.5 = (bf16[512,1024]{1,0:T(8,128)(2,1)S(1)}, bf16[512,1024]{1,0:T(8,128)(2,1)}, u32[]{:S(2)}, u32[]{:S(2)}) collective-permute-start(bf16[512,1024]{1,0:T(8,128)(2,1)S(1)} %collective-permute-done.3), channel_id=1, source_target_pairs={{4,0},{6,2},{8,12},{10,14},{5,1},{7,3},{9,13},{11,15},{20,16},{22,... | collective-permute-start | bytes 3145736 | tf_op jit(solution)/shard_map/ppermute | solution.py:232
  29.3 29.0 %collective-permute-start.8 = (bf16[512,1024]{1,0:T(8,128)(2,1)}, bf16[512,1024]{1,0:T(8,128)(2,1)S(1)}, u32[]{:S(2)}, u32[]{:S(2)}) collective-permute-start(bf16[512,1024]{1,0:T(8,128)(2,1)} %refs_3_.7), channel_id=1, source_target_pairs={{0,2},{2,0},{4,6},{6,4},{8,10},{10,8},{12,14},{14,12},{1,3},{3,1},... | collective-permute-start | bytes 3145736 | tf_op jit(solution)/shard_map/ppermute | solution.py:237
  31.1 1.2 copy-start
  32.4 0.8 copy-start.2
  33.1 25.2 %copy-start.3 = (f32[8192]{0:T(1024)S(1)}, f32[8192]{0:T(1024)}, u32[]{:S(2)}) copy-start(f32[8192]{0:T(1024)} %param.9) | copy-start | bytes 98308
  41.5 36.0 %collective-permute-start.2 = (bf16[512,1024]{1,0:T(8,128)(2,1)}, bf16[512,1024]{1,0:T(8,128)(2,1)}, u32[]{:S(2)}, u32[]{:S(2)}) collective-permute-start(bf16[512,1024]{1,0:T(8,128)(2,1)} %collective-permute-done.1), channel_id=1, source_target_pairs={{4,0},{6,2},{8,12},{10,14},{5,1},{7,3},{9,13},{11,15},{20,16},{22,... | collective-permute-start | bytes 3145736 | tf_op jit(solution)/shard_map/ppermute | solution.py:232
  43.0 37.5 %collective-permute-start.7 = (bf16[512,1024]{1,0:T(8,128)(2,1)S(1)}, bf16[512,1024]{1,0:T(8,128)(2,1)S(1)}, u32[]{:S(2)}, u32[]{:S(2)}) collective-permute-start(bf16[512,1024]{1,0:T(8,128)(2,1)S(1)} %collective-permute-done.refs_1_), channel_id=1, source_target_pairs={{0,2},{2,0},{4,6},{6,4},{8,10},{10,8},{12,14},{14,12},{1,3},{3,1},... | collective-permute-start | bytes 3145736 | tf_op jit(solution)/shard_map/ppermute | solution.py:237
  56.7 43.9 %collective-permute-start.6 = (bf16[512,1024]{1,0:T(8,128)(2,1)S(1)}, bf16[512,1024]{1,0:T(8,128)(2,1)S(1)}, u32[]{:S(2)}, u32[]{:S(2)}) collective-permute-start(bf16[512,1024]{1,0:T(8,128)(2,1)S(1)} %broadcast_select_fusion.refs_1_), channel_id=1, source_target_pairs={{0,2},{2,0},{4,6},{6,4},{8,10},{10,8},{12,14},{14,12},{1,3},{3,1},... | collective-permute-start | bytes 3145736 | tf_op jit(solution)/shard_map/ppermute | solution.py:237
  78.9 42.5 %collective-permute-start.4 = (bf16[512,1024]{1,0:T(8,128)(2,1)S(1)}, bf16[512,1024]{1,0:T(8,128)(2,1)S(1)}, u32[]{:S(2)}, u32[]{:S(2)}) collective-permute-start(bf16[512,1024]{1,0:T(8,128)(2,1)S(1)} %broadcast_select_fusion.1.refs_1_), channel_id=1, source_target_pairs={{0,2},{2,0},{4,6},{6,4},{8,10},{10,8},{12,14},{14,12},{1,3},{3,1},... | collective-permute-start | bytes 3145736 | tf_op jit(solution)/shard_map/ppermute | solution.py:237
  121.3 14.0 %copy-start.6 = (f32[16,1024]{1,0:T(8,128)S(1)}, f32[16,1024]{1,0:T(8,128)}, u32[]{:S(2)}) copy-start(f32[16,1024]{1,0:T(8,128)} %param.12) | copy-start | bytes 196612
  121.3 14.0 %copy-start.7 = (f32[16,1024]{1,0:T(8,128)S(1)}, f32[16,1024]{1,0:T(8,128)}, u32[]{:S(2)}) copy-start(f32[16,1024]{1,0:T(8,128)} %param.13) | copy-start | bytes 196612
  121.3 14.0 %copy-start.5 = (f32[3,7,1024]{2,1,0:T(8,128)S(1)}, f32[3,7,1024]{2,1,0:T(8,128)}, u32[]{:S(2)}) copy-start(f32[3,7,1024]{2,1,0:T(8,128)} %param.11) | copy-start | bytes 258052
  121.3 14.9 %copy-start.4 = (f32[1024]{0:T(1024)S(1)}, f32[1024]{0:T(1024)}, u32[]{:S(2)}) copy-start(f32[1024]{0:T(1024)} %param.14) | copy-start | bytes 12292
  134.0 2.2 collective-permute-start.9
  148.0 3.2 %collective-permute-start.10 = (f32[16,8,128]{2,1,0:T(8,128)S(1)}, f32[16,8,128]{2,1,0:T(8,128)S(1)}, u32[]{:S(2)}, u32[]{:S(2)}) collective-permute-start(f32[16,8,128]{2,1,0:T(8,128)S(1)} %get-tuple-element.29), channel_id=1, source_target_pairs={{0,1},{2,3},{4,5},{6,7},{8,9},{10,11},{12,13},{14,15},{16,17},{18,... | collective-permute-start | bytes 196616 | tf_op jit(solution)/shard_map/ppermute | solution.py:18
  158.5 25.5 %collective-permute-start.11 = (bf16[512,1024]{1,0:T(8,128)(2,1)S(1)}, bf16[512,1024]{1,0:T(8,128)(2,1)S(1)}, u32[]{:S(2)}, u32[]{:S(2)}) collective-permute-start(bf16[512,1024]{1,0:T(8,128)(2,1)S(1)} %piece.11), channel_id=1, source_target_pairs={{0,2},{2,0},{4,6},{6,4},{8,10},{10,8},{12,14},{14,12},{1,3},{3,1},... | collective-permute-start | bytes 3145736 | tf_op jit(solution)/shard_map/ppermute | solution.py:237
  186.8 28.1 %collective-permute-start.15 = (bf16[512,1024]{1,0:T(8,128)(2,1)S(1)}, bf16[512,1024]{1,0:T(8,128)(2,1)S(1)}, u32[]{:S(2)}, u32[]{:S(2)}) collective-permute-start(bf16[512,1024]{1,0:T(8,128)(2,1)S(1)} %piece.12), channel_id=1, source_target_pairs={{0,4},{2,6},{12,8},{14,10},{1,5},{3,7},{13,9},{15,11},{16,20},{18,... | collective-permute-start | bytes 3145736 | tf_op jit(solution)/shard_map/ppermute | solution.py:232
  192.8 24.4 %collective-permute-start.12 = (bf16[512,1024]{1,0:T(8,128)(2,1)S(1)}, bf16[512,1024]{1,0:T(8,128)(2,1)S(1)}, u32[]{:S(2)}, u32[]{:S(2)}) collective-permute-start(bf16[512,1024]{1,0:T(8,128)(2,1)S(1)} %piece.10), channel_id=1, source_target_pairs={{0,2},{2,0},{4,6},{6,4},{8,10},{10,8},{12,14},{14,12},{1,3},{3,1},... | collective-permute-start | bytes 3145736 | tf_op jit(solution)/shard_map/ppermute | solution.py:237
  220.0 23.2 %collective-permute-start.18 = (bf16[512,1024]{1,0:T(8,128)(2,1)S(1)}, bf16[512,1024]{1,0:T(8,128)(2,1)S(1)}, u32[]{:S(2)}, u32[]{:S(2)}) collective-permute-start(bf16[512,1024]{1,0:T(8,128)(2,1)S(1)} %piece.13), channel_id=1, source_target_pairs={{0,4},{2,6},{12,8},{14,10},{1,5},{3,7},{13,9},{15,11},{16,20},{18,... | collective-permute-start | bytes 3145736 | tf_op jit(solution)/shard_map/ppermute | solution.py:232
  224.8 19.7 %collective-permute-start.16 = (bf16[512,1024]{1,0:T(8,128)(2,1)S(1)}, bf16[512,1024]{1,0:T(8,128)(2,1)S(1)}, u32[]{:S(2)}, u32[]{:S(2)}) collective-permute-start(bf16[512,1024]{1,0:T(8,128)(2,1)S(1)} %piece.13), channel_id=1, source_target_pairs={{4,8},{6,10},{8,4},{10,6},{5,9},{7,11},{9,5},{11,7},{20,24},{22,26... | collective-permute-start | bytes 3145736 | tf_op jit(solution)/shard_map/ppermute | solution.py:232
  225.6 23.5 %collective-permute-start.13 = (bf16[512,1024]{1,0:T(8,128)(2,1)S(1)}, bf16[512,1024]{1,0:T(8,128)(2,1)S(1)}, u32[]{:S(2)}, u32[]{:S(2)}) collective-permute-start(bf16[512,1024]{1,0:T(8,128)(2,1)S(1)} %piece.9), channel_id=1, source_target_pairs={{0,2},{2,0},{4,6},{6,4},{8,10},{10,8},{12,14},{14,12},{1,3},{3,1},... | collective-permute-start | bytes 3145736 | tf_op jit(solution)/shard_map/ppermute | solution.py:237
  243.6 32.9 %copy-start.1 = (bf16[512,1024]{1,0:T(8,128)(2,1)S(1)}, bf16[512,1024]{1,0:T(8,128)(2,1)}, u32[]{:S(2)}) copy-start(bf16[512,1024]{1,0:T(8,128)(2,1)} %refs_3_.7) | copy-start | bytes 3145732
  243.7 12.2 %collective-permute-start.19 = (bf16[512,1024]{1,0:T(8,128)(2,1)S(1)}, bf16[512,1024]{1,0:T(8,128)(2,1)S(1)}, u32[]{:S(2)}, u32[]{:S(2)}) collective-permute-start(bf16[512,1024]{1,0:T(8,128)(2,1)S(1)} %add_convert_fusion), channel_id=1, source_target_pairs={{4,8},{6,10},{8,4},{10,6},{5,9},{7,11},{9,5},{11,7},{20,24},{22,26... | collective-permute-start | bytes 3145736 | tf_op jit(solution)/shard_map/ppermute | solution.py:232
  251.9 23.2 %collective-permute-start.17 = (bf16[512,1024]{1,0:T(8,128)(2,1)S(1)}, bf16[512,1024]{1,0:T(8,128)(2,1)S(1)}, u32[]{:S(2)}, u32[]{:S(2)}) collective-permute-start(bf16[512,1024]{1,0:T(8,128)(2,1)S(1)} %piece.14), channel_id=1, source_target_pairs={{0,4},{2,6},{4,0},{6,2},{8,12},{10,14},{12,8},{14,10},{1,5},{3,7},... | collective-permute-start | bytes 3145736 | tf_op jit(solution)/shard_map/ppermute | solution.py:232
  254.3 22.2 %collective-permute-start.14 = (bf16[512,1024]{1,0:T(8,128)(2,1)S(1)}, bf16[512,1024]{1,0:T(8,128)(2,1)S(1)}, u32[]{:S(2)}, u32[]{:S(2)}) collective-permute-start(bf16[512,1024]{1,0:T(8,128)(2,1)S(1)} %piece.8), channel_id=1, source_target_pairs={{0,2},{2,0},{4,6},{6,4},{8,10},{10,8},{12,14},{14,12},{1,3},{3,1},... | collective-permute-start | bytes 3145736 | tf_op jit(solution)/shard_map/ppermute | solution.py:237

commit v3 on v1

v3 whole, which is shorter than its diff:
```python
import functools

import jax
import jax.numpy as jnp
from jax import lax
from jax.experimental import pallas as pl
from jax.experimental.pallas import tpu as pltpu
from jax.sharding import PartitionSpec as P

EPSILON = 1e-06
LANES = 128
MIB = 1024 * 1024


def from_behind(block, axis, distance):
    count = lax.axis_size(axis)
    route = [(i - distance, i) for i in range(count) if i - distance >= 0]
    return lax.ppermute(block, axis, route)


def tree_sum(terms):
    while len(terms) > 1:
        pairs = [terms[i] + terms[i + 1] for i in range(0, len(terms) - 1, 2)]
        terms = pairs + terms[len(pairs) * 2 :]
    return terms[0]


def piece_kernel(place_ref, gated_ref, w_ref, out_ref):
    total = jnp.dot(gated_ref[...], w_ref[...], preferred_element_type=jnp.float32)
    out_ref[...] = total.astype(out_ref.dtype)


def piece(gated, out_weight, place, width, dtype):
    rows, chans = gated.shape
    tile = min(256, width)
    tiles = width // tile
    return pl.pallas_call(
        piece_kernel,
        grid_spec=pltpu.PrefetchScalarGridSpec(
            num_scalar_prefetch=1,
            grid=(tiles,),
            in_specs=[
                pl.BlockSpec((rows, chans), lambda t, p: (0, 0)),
                pl.BlockSpec((chans, tile), lambda t, p: (0, p[0] * tiles + t)),
            ],
            out_specs=pl.BlockSpec((rows, tile), lambda t, p: (0, t)),
        ),
        out_shape=jax.ShapeDtypeStruct((rows, width), dtype),
        compiler_params=pltpu.CompilerParams(vmem_limit_bytes=24 * MIB),
        cost_estimate=pl.CostEstimate(
            flops=2 * rows * chans * width,
            bytes_accessed=2 * chans * width + 2 * rows * chans + 4 * rows * width,
            transcendentals=0,
        ),
        name="piece",
    )(place.astype(jnp.int32)[None], gated, out_weight)


def along_line(block, pairs):
    return lax.ppermute(block, "chan", [(2 * a + y, 2 * b + y) for a, b in pairs for y in (0, 1)])


def across(block, *earlier):
    count = lax.axis_size("chan")
    if earlier:
        block = lax.optimization_barrier((block,) + earlier)[0]
    return lax.ppermute(block, "chan", [(c, c ^ 1) for c in range(count)])


def total(*terms):
    return functools.reduce(lambda a, b: a + b, [t.astype(jnp.float32) for t in terms])


PAIRS = [(0, 1), (1, 0), (2, 3), (3, 2)]
MIDDLE = [(1, 2), (2, 1)]
OUTWARD = [(1, 0), (2, 3)]
INWARD = [(0, 1), (3, 2)]


def gather_and_project(tokens, gain, in_weight):
    me = lax.axis_index("chan")
    depth = tokens.shape[1]
    half = depth // 2
    at_end = (me < 2) | (me >= 6)
    acc = squares = None

    def add(chunk, shard, start=0):
        nonlocal acc, squares
        first, deep = shard * depth + start, chunk.shape[1]
        x = chunk.astype(jnp.float32)
        scaled = (x * lax.dynamic_slice_in_dim(gain, first, deep)).astype(jnp.bfloat16)
        w = lax.dynamic_slice_in_dim(in_weight, first, deep, axis=1)
        part = jnp.einsum("td,kdc->ktc", scaled, w, preferred_element_type=jnp.float32)
        square = jnp.sum(x * x, axis=1, keepdims=True)
        acc = part if acc is None else lax.optimization_barrier(acc + part)
        squares = square if squares is None else squares + square

    own_over = across(tokens)
    next_one = along_line(tokens, PAIRS)
    middle = along_line(tokens, MIDDLE)
    add(tokens, me)
    next_over = across(next_one, own_over)
    second_out = along_line(middle, OUTWARD)
    second_mid = along_line(next_one, MIDDLE)
    add(own_over, me ^ 1)
    add(next_one, me ^ 2)
    second = jnp.where(at_end, second_out, second_mid)
    second_over = across(second, next_over)
    third_out = along_line(second_mid, OUTWARD)
    add(next_over, me ^ 3)
    add(second, me ^ 4)
    third = jnp.where(at_end, third_out, middle)
    third_over = across(third[:, :half], second_over)
    rest_out = along_line(second_over[:, half:], OUTWARD)
    rest_mid = along_line(lax.optimization_barrier((own_over[:, half:], second_mid))[0], MIDDLE)
    add(second_over, me ^ 5)
    add(third, me ^ 6)
    add(jnp.where(at_end, rest_out, rest_mid), me ^ 7, half)
    add(third_over, me ^ 7)
    return acc, squares


def project_and_reduce(gated, out_weight, tokens):
    me = lax.axis_index("chan")
    half = tokens.shape[1] // 2
    send = lambda k, h: piece(gated, out_weight, (me ^ (2 * k + 1)) * 2 + h, half, jnp.bfloat16)
    keep = lambda k, h: piece(gated, out_weight, (me ^ (2 * k)) * 2 + h, half, jnp.float32)
    narrow = lambda a: a.astype(jnp.bfloat16)
    both = (0, 1)

    send_third = [send(3, h) for h in both]
    third_over = across(send_third[0])
    rest_in = along_line(send_third[1], INWARD)
    rest_mid = along_line(send_third[1], MIDDLE)
    third = [narrow(total(keep(3, 0), third_over)), piece(gated, out_weight, (me ^ 6) * 2 + 1, half, jnp.bfloat16)]
    third_in = [along_line(third[0], INWARD), along_line(third[1], INWARD)]
    send_second = [send(2, 0), narrow(total(send(2, 1), rest_in))]
    second_over = [across(send_second[h], third_over) for h in both]
    second = [narrow(total(keep(2, h), second_over[h], third_in[h])) for h in both]
    second_in = [along_line(second[h], INWARD) for h in both]
    second_mid = [along_line(second[h], MIDDLE) for h in both]
    next_over = [across(send(1, h), second_over[h]) for h in both]
    next_one = [narrow(total(keep(1, h), next_over[h], second_mid[h])) for h in both]
    next_in = [along_line(next_one[h], PAIRS) for h in both]
    middle_in = [along_line(narrow(total(third[h], second_in[h])), MIDDLE) for h in both]
    send_own = [send(0, 0), narrow(total(send(0, 1), rest_mid))]
    own_over = [across(send_own[h], next_over[h]) for h in both]
    sums = [total(keep(0, h), own_over[h], next_in[h], middle_in[h]) for h in both]
    return narrow(total(tokens, jnp.concatenate(sums, axis=1)))


def mix_kernel(
    acc_ref, rms_ref, rim_ref, taps_ref, decay_ref, res_ref, skip_ref, q_ref, base_ref, end_ref, win_ref, prod_ref, state_ref
):
    step = pl.program_id(0)
    rows = acc_ref.shape[1]
    groups = taps_ref.shape[2]
    tap_count = taps_ref.shape[1]
    poles = decay_ref.shape[0]
    keep = rim_ref.shape[1]
    unroll = 8

    @pl.when(step == 0)
    def _():
        for g in range(groups):
            win_ref[:, :keep, g, :] = rim_ref[:, :, g * LANES : (g + 1) * LANES]
        state_ref[...] = jnp.zeros_like(state_ref)

    inv_rms = rms_ref[...]
    for i in range(3):
        for g in range(groups):
            cols = acc_ref[i, :, g * LANES : (g + 1) * LANES] * inv_rms
            win_ref[i, keep:, g, :] = cols.astype(jnp.bfloat16).astype(jnp.float32)

    def convolve(blk, nothing):
        first = blk * unroll
        conv = []
        for i in range(3):
            taps = [taps_ref[i, j] for j in range(tap_count)]
            held = [win_ref[i, first + keep - (tap_count - 1) + r] for r in range(unroll + tap_count - 1)]
            conv.append(
                [
                    functools.reduce(
                        lambda a, b: a + b, [taps[j] * held[r + tap_count - 1 - j] for j in range(tap_count)]
                    )
                    for r in range(unroll)
                ]
            )
        for r in range(unroll):
            q_ref[first + r] = conv[0][r]
            prod_ref[first + r] = conv[1][r] * conv[2][r]
        return nothing

    lax.fori_loop(0, rows // unroll, convolve, 0)
    win_ref[:, :keep] = win_ref[:, rows:]
    decay = [jnp.exp(decay_ref[n]) for n in range(poles)]
    res = [res_ref[n] for n in range(poles)]
    skip = skip_ref[0]

    def recur(blk, state):
        state = list(state)
        for r in range(unroll):
            t = blk * unroll + r
            product = prod_ref[t]
            terms = [skip * product]
            for n in range(poles):
                state[n] = decay[n] * state[n] + product
                terms.append(res[n] * state[n])
            base_ref[t] = q_ref[t] * tree_sum(terms)
        return tuple(state)

    state = lax.fori_loop(0, rows // unroll, recur, tuple(state_ref[n] for n in range(poles)))
    for n in range(poles):
        state_ref[n] = state[n]

    @pl.when(step == pl.num_programs(0) - 1)
    def _():
        for n in range(poles):
            end_ref[n] = state[n]


def mix(acc, inv_rms, rim, taps, log_decay, residue, skip):
    rows, chans = acc.shape[1:]
    groups = chans // LANES
    tap_count, poles = taps.shape[1], log_decay.shape[0]
    keep = rim.shape[1]
    blk = min(128, rows)
    whole = lambda *shape: pl.BlockSpec(shape, lambda t: (0,) * len(shape))
    row_spec = pl.BlockSpec((blk, groups, LANES), lambda t: (t, 0, 0))
    return pl.pallas_call(
        mix_kernel,
        grid=(rows // blk,),
        in_specs=[
            pl.BlockSpec((3, blk, chans), lambda t: (0, t, 0)),
            pl.BlockSpec((blk, 1), lambda t: (t, 0)),
            whole(3, keep, chans),
            whole(3, tap_count, groups, LANES),
            whole(poles, groups, LANES),
            whole(poles, groups, LANES),
            whole(1, groups, LANES),
        ],
        out_specs=[row_spec, row_spec, whole(poles, groups, LANES)],
        out_shape=[
            jax.ShapeDtypeStruct((rows, groups, LANES), jnp.float32),
            jax.ShapeDtypeStruct((rows, groups, LANES), jnp.float32),
            jax.ShapeDtypeStruct((poles, groups, LANES), jnp.float32),
        ],
        scratch_shapes=[
            pltpu.VMEM((3, keep + blk, groups, LANES), jnp.float32),
            pltpu.VMEM((blk, groups, LANES), jnp.float32),
            pltpu.VMEM((poles, groups, LANES), jnp.float32),
        ],
        compiler_params=pltpu.CompilerParams(vmem_limit_bytes=32 * MIB),
        cost_estimate=pl.CostEstimate(
            flops=110 * rows * groups * LANES, bytes_accessed=20 * rows * groups * LANES, transcendentals=0
        ),
        name="mix",
    )(acc, inv_rms, rim, taps, log_decay, residue, skip)


def carry_kernel(q_ref, base_ref, state_ref, decay_ref, res_ref, out_ref, coef_ref, row_ref):
    step = pl.program_id(0)
    rows, groups = q_ref.shape[:2]
    poles = decay_ref.shape[0]
    decay = [jnp.exp(decay_ref[n]) for n in range(poles)]

    @pl.when(step == 0)
    def _():
        for n in range(poles):
            coef_ref[n] = res_ref[n] * (decay[n] * state_ref[n])

    unroll = 8

    def body(blk, coef):
        coef = list(coef)
        for r in range(unroll):
            t = blk * unroll + r
            row_ref[t] = base_ref[t] + q_ref[t] * tree_sum(list(coef))
            for n in range(poles):
                coef[n] = decay[n] * coef[n]
        return tuple(coef)

    coef = lax.fori_loop(0, rows // unroll, body, tuple(coef_ref[n] for n in range(poles)))
    for n in range(poles):
        coef_ref[n] = coef[n]
    for g in range(groups):
        out_ref[:, g * LANES : (g + 1) * LANES] = row_ref[:, g, :].astype(jnp.bfloat16)


def carry(query, base, state, log_decay, residue):
    rows, groups = query.shape[:2]
    poles = log_decay.shape[0]
    blk = min(128, rows)
    whole = lambda *shape: pl.BlockSpec(shape, lambda t: (0,) * len(shape))
    row_spec = pl.BlockSpec((blk, groups, LANES), lambda t: (t, 0, 0))
    return pl.pallas_call(
        carry_kernel,
        grid=(rows // blk,),
        in_specs=[row_spec, row_spec] + [whole(poles, groups, LANES)] * 3,
        out_specs=pl.BlockSpec((blk, groups * LANES), lambda t: (t, 0)),
        out_shape=jax.ShapeDtypeStruct((rows, groups * LANES), jnp.bfloat16),
        scratch_shapes=[
            pltpu.VMEM((poles, groups, LANES), jnp.float32),
            pltpu.VMEM((blk, groups, LANES), jnp.float32),
        ],
        compiler_params=pltpu.CompilerParams(vmem_limit_bytes=48 * MIB),
        cost_estimate=pl.CostEstimate(
            flops=40 * rows * groups * LANES, bytes_accessed=10 * rows * groups * LANES, transcendentals=0
        ),
        name="carry",
    )(query, base, state, log_decay, residue)


def per_device(tokens, norm_gain, in_weight, short_weight, log_decay, residue, skip, out_weight):
    rows, chans = tokens.shape
    groups = chans // LANES
    by_lane = lambda a: a.reshape(a.shape[:-1] + (groups, LANES))
    taps, log_decay, residue = by_lane(short_weight), by_lane(log_decay), by_lane(residue)
    skip = by_lane(skip[None, :])

    model_width, keep = norm_gain.shape[0], 8
    paired_line = lax.axis_size("chan") == 8
    if paired_line:
        acc, squares = gather_and_project(tokens, norm_gain, in_weight)
    else:
        gathered = lax.all_gather(tokens, "chan", axis=1, tiled=True).astype(jnp.float32)
        squares = jnp.sum(gathered * gathered, axis=1, keepdims=True)
        scaled = (gathered * norm_gain[None, :]).astype(jnp.bfloat16)
        acc = jnp.einsum("td,kdc->ktc", scaled, in_weight, preferred_element_type=jnp.float32)
    inv_rms = lax.rsqrt(squares / model_width + EPSILON)
    rim = (acc[:, rows - keep :] * inv_rms[None, rows - keep :]).astype(jnp.bfloat16)
    rim = from_behind(rim, "seq", 1).astype(jnp.float32)
    query, base, end = mix(acc, inv_rms, rim, taps, log_decay, residue, skip)
    shard_decay = jnp.exp(rows * log_decay)
    state, passing = jnp.zeros_like(end), end
    for _ in range(lax.axis_size("seq") - 1):
        passing = from_behind(passing, "seq", 1)
        state = state + passing
        passing = passing * shard_decay
    gated = carry(query, base, state, log_decay, residue)
    if paired_line:
        return project_and_reduce(gated, out_weight, tokens)
    partial = jnp.dot(gated, out_weight, preferred_element_type=jnp.float32)
    branch = lax.psum_scatter(partial.astype(jnp.bfloat16), "chan", scatter_dimension=1, tiled=True)
    return (tokens.astype(jnp.float32) + branch.astype(jnp.float32)).astype(jnp.bfloat16)


def solution(mesh):
    return jax.shard_map(
        per_device,
        mesh=mesh,
        in_specs=(
            P(("groups", "seq"), "chan"),
            P(),
            P(None, None, "chan"),
            P(None, None, "chan"),
            P(None, "chan"),
            P(None, "chan"),
            P("chan"),
            P("chan", None),
        ),
        out_specs=P(("groups", "seq"), "chan"),
        check_vma=False,
    )
```

time: 385 us -> 266 us (0.69)
  waiting for transfers between devices: 281 us -> 74.4 us
  starting transfers between devices: 3.63 us -> 55.1 us
  matrix products: 16.8 us -> 47.9 us
  Pallas kernels: 65.7 us -> 36.7 us
  local copies, waits for them, and re-layouts: 1.72 us -> 28.7 us
  other arithmetic: 2.59 us -> 21.2 us
  between operations: 13.5 us -> 0.71 us
    reduce_scatter x1 -> x0, waiting for transfers between devices: 148 us -> none  [per_device(): lax.psum_scatter(partial.astype(jnp.bfloat16), 'chan', scatter_dimension=...]
    all_gather x1 -> x0, waiting for transfers between devices: 130 us -> none  [per_device(): gathered = lax.all_gather(tokens, 'chan', axis=1, tiled=True)]
    ppermute x0 -> x30, waiting for transfers between devices: none -> 72.9 us  [the longest x11 57.7 us: across(): return lax.ppermute(block, 'chan', [(c, c ^ 1) for c in range(count)])]
    ppermute x0 -> x30, starting transfers between devices: none -> 51.6 us  [the longest x19 35.3 us: along_line(): lax.ppermute(block, 'chan', [(2 * a + y, 2 * b + y) for a, b in pairs for...]
    dot_general x1 -> x9, matrix products: 16.8 us -> 47.9 us  [add(): jnp.einsum('td,kdc->ktc', scaled, w, preferred_element_type=jnp.float32)]
    pallas_call x1 -> x16, Pallas kernels: 49.3 us -> 18.6 us  [piece(): pl.pallas_call(piece_kernel, grid_spec=pltpu.PrefetchScalarGridSpec(num_s...]
    unnamed x14 -> x38, local copies, waits for them, and re-layouts: 0.81 us -> 25.7 us
    convert_element_type x1 -> x12, other arithmetic: 2.59 us -> 9.49 us  [the longest x10 9.4 us: project_and_reduce(): narrow = lambda a: a.astype(jnp.bfloat16)]
  transfers between devices with their start and end apart: 4 -> 32, of which waited for: 4 -> 15; matrix products, arithmetic and copies ran while one was open for 0% -> 24% of each run, Pallas kernels for 0% -> 6%
where the time goes in v3:
time: 266 us; the launch traced here: 265 us
  waiting for transfers between devices  74.4 us (28%)
  starting transfers between devices  55.1 us (21%)
  matrix products  47.9 us (18%)
  Pallas kernels  36.7 us (14%)
  local copies, waits for them, and re-layouts  28.7 us (11%)
  other arithmetic  21.2 us (8%)
    ppermute x11, waiting for transfers between devices, across(): return lax.ppermute(block, 'chan', [(c, c ^ 1) for c in range(count)])  57.7 us
    dot_general x9, matrix products, add(): jnp.einsum('td,kdc->ktc', scaled, w, preferred_element_type=jnp.float32)  47.9 us
    ppermute x19, starting transfers between devices, along_line(): lax.ppermute(block, 'chan', [(2 * a + y, 2 * b + y) for a, b in pairs for...  35.3 us
    unnamed x38, local copies, waits for them, and re-layouts  25.7 us
    pallas_call x16, Pallas kernels, piece(): pl.pallas_call(piece_kernel, grid_spec=pltpu.PrefetchScalarGridSpec(num_s...  18.6 us
    ppermute x11, starting transfers between devices, across(): return lax.ppermute(block, 'chan', [(c, c ^ 1) for c in range(count)])  16.3 us
    ppermute x19, waiting for transfers between devices, along_line(): lax.ppermute(block, 'chan', [(2 * a + y, 2 * b + y) for a, b in pairs for...  15.2 us
    pallas_call x1, Pallas kernels, mix(): pl.pallas_call(mix_kernel, grid=(rows // blk,), in_specs=[pl.BlockSpec((3...  13.4 us
  transfers between devices with their start and end apart: 32, of which 15 were waited for; matrix products, arithmetic and copies ran while one was open for 24% of the time, Pallas kernels for 6%

profile of v3, /device:TPU:0, one launch (start us, length us, event | category | flops | bytes accessed | tf_op | source)
XLA Modules:
  0.0 264.6 jit_solution(10706935268710514420)
XLA Ops:
  0.0 3.0 %collective-permute-start = (bf16[512,1024]{1,0:T(8,128)(2,1)}, bf16[512,1024]{1,0:T(8,128)(2,1)S(1)}, u32[]{:S(2)}, u32[]{:S(2)}) collective-permute-start(bf16[512,1024]{1,0:T(8,128)(2,1)} %param.8), channel_id=1, source_target_pairs={{0,2},{2,0},{4,6},{6,4},{8,10},{10,8},{12,14},{14,12},{1,3},{3,1},... | collective-permute-start | bytes 3145736 | tf_op jit(solution)/shard_map/ppermute | solution.py:67
  7.8 5.9 %fusion.12 = f32[3,1024,512]{1,2,0:T(8,128)S(1)} fusion(bf16[3,8192,1024]{2,1,0:T(8,128)(2,1)} %param.10, s32[]{:T(128)S(6)} %select_n.56, bf16[512,1024]{1,0:T(8,128)(2,1)} %param.8, f32[1024]{0:T(1024)S(1)} %get-tuple-element.43), kind=kOutput, calls=%fused_computation.20 | convolution fusion | flops 3222798336 | bytes 13635588 | tf_op jit(solution)/shard_map/td,kdc->ktc/dot_general | solution.py:93
  14.0 12.3 %collective-permute-done = bf16[512,1024]{1,0:T(8,128)(2,1)S(1)} collective-permute-done((bf16[512,1024]{1,0:T(8,128)(2,1)}, bf16[512,1024]{1,0:T(8,128)(2,1)S(1)}, u32[]{:S(2)}, u32[]{:S(2)}) %collective-permute-start) | collective-permute-done | bytes 1048608 | tf_op jit(solution)/shard_map/ppermute | solution.py:67
  26.3 5.9 %add_bitcast_fusion = f32[3,512,1024]{2,1,0:T(8,128)S(1)} fusion(f32[3,1024,512]{1,2,0:T(8,128)S(1)} %fusion.12, bf16[3,8192,1024]{2,1,0:T(8,128)(2,1)} %param.10, s32[]{:T(128)S(6)} %select_n.57, bf16[512,1024]{1,0:T(8,128)(2,1)S(1)} %collective-permute-done, f32[1024]{0:T(1024)S(1)} %get-tuple-element.42), kind=kOutput, calls=%fused_computation.17 | convolution fusion | flops 3224371200 | bytes 19927044 | tf_op jit(solution)/shard_map/td,kdc->ktc/dot_general | solution.py:93
  34.1 5.8 %fusion.8 = f32[3,1024,512]{1,2,0:T(8,128)S(1)} fusion(bf16[3,8192,1024]{2,1,0:T(8,128)(2,1)} %param.10, s32[]{:T(128)S(6)} %select_n.58, bf16[512,1024]{1,0:T(8,128)(2,1)} %collective-permute-done.1, f32[1024]{0:T(1024)S(1)} %get-tuple-element.41), kind=kOutput, calls=%fused_computation.15 | convolution fusion | flops 3222798336 | bytes 13635588 | tf_op jit(solution)/shard_map/td,kdc->ktc/dot_general | solution.py:93
  39.9 2.2 bitcast_add_fusion.6
  48.2 8.9 %collective-permute-done.2 = bf16[512,1024]{1,0:T(8,128)(2,1)} collective-permute-done((bf16[512,1024]{1,0:T(8,128)(2,1)}, bf16[512,1024]{1,0:T(8,128)(2,1)}, u32[]{:S(2)}, u32[]{:S(2)}) %collective-permute-start.2) | collective-permute-done | bytes 1048608 | tf_op jit(solution)/shard_map/ppermute | solution.py:67
  57.1 5.8 %bitcast_add_fusion.5 = f32[3,512,1024]{2,1,0:T(8,128)S(1)} fusion(f32[3,512,1024]{2,1,0:T(8,128)S(1)} %bitcast_add_fusion.6, bf16[3,8192,1024]{2,1,0:T(8,128)(2,1)} %param.10, s32[]{:T(128)S(6)} %select_n.59, bf16[512,1024]{1,0:T(8,128)(2,1)} %collective-permute-done.2, f32[1024]{0:T(1024)S(1)} %get-tuple-element.40), kind=kOutput, calls=%fused_computation.5 | convolution fusion | flops 3224371200 | bytes 19927044 | tf_op jit(solution)/shard_map/td,kdc->ktc/dot_general | solution.py:93
  63.0 8.6 %collective-permute-done.4 = bf16[512,1024]{1,0:T(8,128)(2,1)S(1)} collective-permute-done((bf16[512,1024]{1,0:T(8,128)(2,1)}, bf16[512,1024]{1,0:T(8,128)(2,1)S(1)}, u32[]{:S(2)}, u32[]{:S(2)}) %collective-permute-start.4) | collective-permute-done | bytes 1048608 | tf_op jit(solution)/shard_map/ppermute | solution.py:60
  72.6 5.6 %bitcast_add_fusion.4 = f32[3,512,1024]{2,1,0:T(8,128)S(1)} fusion(f32[3,512,1024]{2,1,0:T(8,128)S(1)} %bitcast_add_fusion.5, bf16[3,8192,1024]{2,1,0:T(8,128)(2,1)} %param.10, s32[]{:T(128)S(6)} %select_n.60, bf16[512,1024]{1,0:T(8,128)(2,1)S(1)} %get-tuple-element.19, f32[1024]{0:T(1024)S(1)} %get-tuple-element.39), kind=kOutput, calls=%fused_computation.4 | convolution fusion | flops 3224371200 | bytes 19927044 | tf_op jit(solution)/shard_map/td,kdc->ktc/dot_general | solution.py:93
  81.7 13.3 %collective-permute-done.6 = bf16[512,1024]{1,0:T(8,128)(2,1)S(1)} collective-permute-done((bf16[512,1024]{1,0:T(8,128)(2,1)S(1)}, bf16[512,1024]{1,0:T(8,128)(2,1)S(1)}, u32[]{:S(2)}, u32[]{:S(2)}) %collective-permute-start.6) | collective-permute-done | bytes 1048608 | tf_op jit(solution)/shard_map/ppermute | solution.py:67
  95.0 5.6 %bitcast_add_fusion.3 = f32[3,512,1024]{2,1,0:T(8,128)S(1)} fusion(f32[3,512,1024]{2,1,0:T(8,128)S(1)} %bitcast_add_fusion.4, bf16[3,8192,1024]{2,1,0:T(8,128)(2,1)} %param.10, s32[]{:T(128)S(6)} %select_n.63, bf16[512,1024]{1,0:T(8,128)(2,1)S(1)} %collective-permute-done.6, f32[1024]{0:T(1024)S(1)} %get-tuple-element.38), kind=kOutput, calls=%fused_computation.3 | convolution fusion | flops 3224371200 | bytes 19927044 | tf_op jit(solution)/shard_map/td,kdc->ktc/dot_general | solution.py:93
  102.2 2.5 collective-permute-done.7
  105.1 5.6 %bitcast_add_fusion.2 = f32[3,512,1024]{2,1,0:T(8,128)S(1)} fusion(f32[3,512,1024]{2,1,0:T(8,128)S(1)} %bitcast_add_fusion.3, bf16[3,8192,1024]{2,1,0:T(8,128)(2,1)} %param.10, s32[]{:T(128)S(6)} %select_n.64, bf16[512,1024]{1,0:T(8,128)(2,1)S(1)} %get-tuple-element.34, f32[1024]{0:T(1024)S(1)} %get-tuple-element.37), kind=kOutput, calls=%fused_computation.2 | convolution fusion | flops 3224371200 | bytes 19927044 | tf_op jit(solution)/shard_map/td,kdc->ktc/dot_general | solution.py:93
  110.8 2.6 collective-permute-start.10
  114.6 3.8 %bitcast_add_fusion.1 = f32[3,512,1024]{2,1,0:T(8,128)S(1)} fusion(f32[3,512,1024]{2,1,0:T(8,128)S(1)} %bitcast_add_fusion.2, bf16[3,8192,1024]{2,1,0:T(8,128)(2,1)} %param.10, s32[]{:T(128)S(6)} %select_n.66, f32[512]{0:T(512)S(1)} %get-tuple-element.36, bf16[512,512]{1,0:T(8,128)(2,1)S(1)} %collective-permute-done.8, ...), kind=kOutput, calls=%fused_computation.1 | convolution fusion | flops 1613234176 | bytes 16779268 | tf_op jit(solution)/shard_map/td,kdc->ktc/dot_general | solution.py:93
  120.5 3.8 %bitcast_add_fusion.acc_ref = f32[3,512,1024]{2,1,0:T(8,128)S(1)} fusion(f32[3,512,1024]{2,1,0:T(8,128)S(1)} %bitcast_add_fusion.1, bf16[3,8192,1024]{2,1,0:T(8,128)(2,1)} %param.10, s32[]{:T(128)S(6)} %select_n.69, bf16[512,512]{1,0:T(8,128)(2,1)S(1)} %collective-permute-done.10, f32[512]{0:T(512)S(1)} %get-tuple-element.35), kind=kOutput, calls=%fused_computation | convolution fusion | flops 1612972032 | bytes 16254980 | tf_op jit(solution)/shard_map/td,kdc->ktc/dot_general | solution.py:93
  125.0 2.6 copy-done.3
  129.8 2.8 %copy-done.4 = f32[3,512,1024]{2,1,0:T(8,128)S(1)} copy-done((f32[3,512,1024]{2,1,0:T(8,128)S(1)}, f32[3,512,1024]{2,1,0:T(8,128)}, u32[]{:S(2)}) %copy-start.4) | copy-done | bytes 6291480
  132.6 13.4 %mix.1 = (f32[512,8,128]{2,1,0:T(8,128)S(1)}, f32[512,8,128]{2,1,0:T(8,128)S(1)}, f32[16,8,128]{2,1,0:T(8,128)S(1)}) custom-call(f32[3,512,1024]{2,1,0:T(8,128)S(1)} %copy-done.4, f32[512,1]{1,0:T(8,128)S(1)} %copy.45.rms_ref, f32[3,8,1024]{2,1,0:T(8,128)S(1)} %convert_element_type.179.rim_ref, f32[3,7,8,128]{3,2,1,0:T(8,128)S(1)} %reshape.103.taps_ref, ...), custom_call_target="tpu_custom_call" | custom-call | flops 57671680 | bytes 10485760 | tf_op jit(solution)/shard_map/mix/pallas_call | solution.py:230
  147.3 2.2 collective-permute-start.12
  152.1 4.7 %carry.1.gated_ref = bf16[512,1024]{1,0:T(8,128)(2,1)S(1)} custom-call(f32[512,8,128]{2,1,0:T(8,128)S(1)} %get-tuple-element.22.q_ref, f32[512,8,128]{2,1,0:T(8,128)S(1)} %copy-done.6, f32[16,8,128]{2,1,0:T(8,128)S(1)} %collective-permute-done.12.state_ref, f32[16,8,128]{2,1,0:T(8,128)S(1)} %bitcast.68, f32[16,8,128]{2,1,0:T(8,128)S(1)} %bitcast.70), custom_call_target="tpu_custom_call" | custom-call | flops 20971520 | bytes 5242880 | tf_op jit(solution)/shard_map/carry/pallas_call | solution.py:296
  156.7 5.8 %copy-done = bf16[1024,8192]{1,0:T(8,128)(2,1)S(1)} copy-done((bf16[1024,8192]{1,0:T(8,128)(2,1)S(1)}, bf16[1024,8192]{1,0:T(8,128)(2,1)}, u32[]{:S(2)}) %copy-start) | copy-done | bytes 16777240
  166.3 5.8 %copy-done.1 = bf16[1024,8192]{1,0:T(8,128)(2,1)S(1)} copy-done((bf16[1024,8192]{1,0:T(8,128)(2,1)S(1)}, bf16[1024,8192]{1,0:T(8,128)(2,1)}, u32[]{:S(2)}) %copy-start.1) | copy-done | bytes 16777240
  174.6 4.9 %collective-permute-start.23 = (bf16[512,512]{1,0:T(8,128)(2,1)S(1)}, bf16[512,512]{1,0:T(8,128)(2,1)}, u32[]{:S(2)}, u32[]{:S(2)}) collective-permute-start(bf16[512,512]{1,0:T(8,128)(2,1)S(1)} %piece.26), channel_id=1, source_target_pairs={{0,4},{2,6},{12,8},{14,10},{1,5},{3,7},{13,9},{15,11},{16,20},{18,... | collective-permute-start | bytes 1572872 | tf_op jit(solution)/shard_map/ppermute | solution.py:60
  205.8 6.7 %collective-permute-start.20 = (bf16[512,512]{1,0:T(8,128)(2,1)S(1)}, bf16[512,512]{1,0:T(8,128)(2,1)S(1)}, u32[]{:S(2)}, u32[]{:S(2)}) collective-permute-start(bf16[512,512]{1,0:T(8,128)(2,1)S(1)} %add_convert_fusion.7), channel_id=1, source_target_pairs={{0,4},{2,6},{12,8},{14,10},{1,5},{3,7},{13,9},{15,11},{16,20},{18,... | collective-permute-start | bytes 1572872 | tf_op jit(solution)/shard_map/ppermute | solution.py:60
  212.4 2.4 collective-permute-done.27
  216.8 5.7 %collective-permute-start.30 = (bf16[512,512]{1,0:T(8,128)(2,1)S(1)}, bf16[512,512]{1,0:T(8,128)(2,1)S(1)}, u32[]{:S(2)}, u32[]{:S(2)}) collective-permute-start(bf16[512,512]{1,0:T(8,128)(2,1)S(1)} %add_convert_fusion.2), channel_id=1, source_target_pairs={{0,4},{2,6},{12,8},{14,10},{1,5},{3,7},{13,9},{15,11},{16,20},{18,... | collective-permute-start | bytes 1572872 | tf_op jit(solution)/shard_map/ppermute | solution.py:60
  222.5 2.8 %collective-permute-done.15 = bf16[512,512]{1,0:T(8,128)(2,1)S(1)} collective-permute-done((bf16[512,512]{1,0:T(8,128)(2,1)S(1)}, bf16[512,512]{1,0:T(8,128)(2,1)S(1)}, u32[]{:S(2)}, u32[]{:S(2)}) %collective-permute-start.15) | collective-permute-done | bytes 524320 | tf_op jit(solution)/shard_map/ppermute | solution.py:67
  229.5 10.6 %collective-permute-done.25 = bf16[512,512]{1,0:T(8,128)(2,1)S(1)} collective-permute-done((bf16[512,512]{1,0:T(8,128)(2,1)S(1)}, bf16[512,512]{1,0:T(8,128)(2,1)S(1)}, u32[]{:S(2)}, u32[]{:S(2)}) %collective-permute-start.25) | collective-permute-done | bytes 524320 | tf_op jit(solution)/shard_map/ppermute | solution.py:67
  244.6 6.7 %collective-permute-done.16 = bf16[512,512]{1,0:T(8,128)(2,1)S(1)} collective-permute-done((bf16[512,512]{1,0:T(8,128)(2,1)S(1)}, bf16[512,512]{1,0:T(8,128)(2,1)S(1)}, u32[]{:S(2)}, u32[]{:S(2)}) %collective-permute-start.16) | collective-permute-done | bytes 524320 | tf_op jit(solution)/shard_map/ppermute | solution.py:67
  252.1 5.8 %copy-done.2 = bf16[1024,8192]{1,0:T(8,128)(2,1)S(1)} copy-done((bf16[1024,8192]{1,0:T(8,128)(2,1)S(1)}, bf16[1024,8192]{1,0:T(8,128)(2,1)}, u32[]{:S(2)}) %copy-start.2) | copy-done | bytes 16777240
  (131 shorter events, 79.8 us)
Async XLA Ops:
  0.0 26.3 %collective-permute-start = (bf16[512,1024]{1,0:T(8,128)(2,1)}, bf16[512,1024]{1,0:T(8,128)(2,1)S(1)}, u32[]{:S(2)}, u32[]{:S(2)}) collective-permute-start(bf16[512,1024]{1,0:T(8,128)(2,1)} %param.8), channel_id=1, source_target_pairs={{0,2},{2,0},{4,6},{6,4},{8,10},{10,8},{12,14},{14,12},{1,3},{3,1},... | collective-permute-start | bytes 3145736 | tf_op jit(solution)/shard_map/ppermute | solution.py:67
  3.0 29.3 %collective-permute-start.1 = (bf16[512,1024]{1,0:T(8,128)(2,1)}, bf16[512,1024]{1,0:T(8,128)(2,1)}, u32[]{:S(2)}, u32[]{:S(2)}) collective-permute-start(bf16[512,1024]{1,0:T(8,128)(2,1)} %param.8), channel_id=1, source_target_pairs={{0,4},{2,6},{4,0},{6,2},{8,12},{10,14},{12,8},{14,10},{1,5},{3,7},... | collective-permute-start | bytes 3145736 | tf_op jit(solution)/shard_map/ppermute | solution.py:60
  4.5 39.4 %collective-permute-start.3 = (bf16[512,1024]{1,0:T(8,128)(2,1)}, bf16[512,1024]{1,0:T(8,128)(2,1)}, u32[]{:S(2)}, u32[]{:S(2)}) collective-permute-start(bf16[512,1024]{1,0:T(8,128)(2,1)} %param.8), channel_id=1, source_target_pairs={{4,8},{6,10},{8,4},{10,6},{5,9},{7,11},{9,5},{11,7},{20,24},{22,26... | collective-permute-start | bytes 3145736 | tf_op jit(solution)/shard_map/ppermute | solution.py:60
  32.3 24.8 %collective-permute-start.2 = (bf16[512,1024]{1,0:T(8,128)(2,1)}, bf16[512,1024]{1,0:T(8,128)(2,1)}, u32[]{:S(2)}, u32[]{:S(2)}) collective-permute-start(bf16[512,1024]{1,0:T(8,128)(2,1)} %collective-permute-done.1), channel_id=1, source_target_pairs={{0,2},{2,0},{4,6},{6,4},{8,10},{10,8},{12,14},{14,12},{1,3},{3,1},... | collective-permute-start | bytes 3145736 | tf_op jit(solution)/shard_map/ppermute | solution.py:67
  42.1 20.9 %collective-permute-start.5 = (bf16[512,1024]{1,0:T(8,128)(2,1)}, bf16[512,1024]{1,0:T(8,128)(2,1)S(1)}, u32[]{:S(2)}, u32[]{:S(2)}) collective-permute-start(bf16[512,1024]{1,0:T(8,128)(2,1)} %collective-permute-done.1), channel_id=1, source_target_pairs={{4,8},{6,10},{8,4},{10,6},{5,9},{7,11},{9,5},{11,7},{20,24},{22,26... | collective-permute-start | bytes 3145736 | tf_op jit(solution)/shard_map/ppermute | solution.py:60
  43.9 27.6 %collective-permute-start.4 = (bf16[512,1024]{1,0:T(8,128)(2,1)}, bf16[512,1024]{1,0:T(8,128)(2,1)S(1)}, u32[]{:S(2)}, u32[]{:S(2)}) collective-permute-start(bf16[512,1024]{1,0:T(8,128)(2,1)} %collective-permute-done.3), channel_id=1, source_target_pairs={{4,0},{6,2},{8,12},{10,14},{5,1},{7,3},{9,13},{11,15},{20,16},{22,... | collective-permute-start | bytes 3145736 | tf_op jit(solution)/shard_map/ppermute | solution.py:60
  72.0 23.0 %collective-permute-start.6 = (bf16[512,1024]{1,0:T(8,128)(2,1)S(1)}, bf16[512,1024]{1,0:T(8,128)(2,1)S(1)}, u32[]{:S(2)}, u32[]{:S(2)}) collective-permute-start(bf16[512,1024]{1,0:T(8,128)(2,1)S(1)} %get-tuple-element.19), channel_id=1, source_target_pairs={{0,2},{2,0},{4,6},{6,4},{8,10},{10,8},{12,14},{14,12},{1,3},{3,1},... | collective-permute-start | bytes 3145736 | tf_op jit(solution)/shard_map/ppermute | solution.py:67
  78.2 35.5 %collective-permute-start.9 = (bf16[512,512]{1,0:T(8,128)(2,1)S(1)}, bf16[512,512]{1,0:T(8,128)(2,1)S(1)}, u32[]{:S(2)}, u32[]{:S(2)}) collective-permute-start(bf16[512,512]{1,0:T(8,128)(2,1)S(1)} %slice.22), channel_id=1, source_target_pairs={{4,8},{6,10},{8,4},{10,6},{5,9},{7,11},{9,5},{11,7},{20,24},{22,26... | collective-permute-start | bytes 1572872 | tf_op jit(solution)/shard_map/ppermute | solution.py:60
  78.9 25.8 %collective-permute-start.7 = (bf16[512,1024]{1,0:T(8,128)(2,1)S(1)}, bf16[512,1024]{1,0:T(8,128)(2,1)S(1)}, u32[]{:S(2)}, u32[]{:S(2)}) collective-permute-start(bf16[512,1024]{1,0:T(8,128)(2,1)S(1)} %collective-permute-done.5), channel_id=1, source_target_pairs={{4,0},{6,2},{8,12},{10,14},{5,1},{7,3},{9,13},{11,15},{20,16},{22,... | collective-permute-start | bytes 3145736 | tf_op jit(solution)/shard_map/ppermute | solution.py:60
  100.7 14.0 %collective-permute-start.8 = (bf16[512,512]{1,0:T(8,128)(2,1)S(1)}, bf16[512,512]{1,0:T(8,128)(2,1)S(1)}, u32[]{:S(2)}, u32[]{:S(2)}) collective-permute-start(bf16[512,512]{1,0:T(8,128)(2,1)S(1)} %slice.21), channel_id=1, source_target_pairs={{4,0},{6,2},{8,12},{10,14},{5,1},{7,3},{9,13},{11,15},{20,16},{22,... | collective-permute-start | bytes 1572872 | tf_op jit(solution)/shard_map/ppermute | solution.py:60
  110.8 9.8 %collective-permute-start.10 = (bf16[512,512]{1,0:T(8,128)(2,1)S(1)}, bf16[512,512]{1,0:T(8,128)(2,1)S(1)}, u32[]{:S(2)}, u32[]{:S(2)}) collective-permute-start(bf16[512,512]{1,0:T(8,128)(2,1)S(1)} %slice.23), channel_id=1, source_target_pairs={{0,2},{2,0},{4,6},{6,4},{8,10},{10,8},{12,14},{14,12},{1,3},{3,1},... | collective-permute-start | bytes 1572872 | tf_op jit(solution)/shard_map/ppermute | solution.py:67
  127.6 2.1 collective-permute-start.11
  147.3 3.1 %collective-permute-start.12 = (f32[16,8,128]{2,1,0:T(8,128)S(1)}, f32[16,8,128]{2,1,0:T(8,128)S(1)}, u32[]{:S(2)}, u32[]{:S(2)}) collective-permute-start(f32[16,8,128]{2,1,0:T(8,128)S(1)} %get-tuple-element.24), channel_id=1, source_target_pairs={{0,1},{2,3},{4,5},{6,7},{8,9},{10,11},{12,13},{14,15},{16,17},{18,... | collective-permute-start | bytes 196616 | tf_op jit(solution)/shard_map/ppermute | solution.py:18
  164.3 22.2 %collective-permute-start.13 = (bf16[512,512]{1,0:T(8,128)(2,1)}, bf16[512,512]{1,0:T(8,128)(2,1)}, u32[]{:S(2)}, u32[]{:S(2)}) collective-permute-start(bf16[512,512]{1,0:T(8,128)(2,1)} %piece.20), channel_id=1, source_target_pairs={{0,2},{2,0},{4,6},{6,4},{8,10},{10,8},{12,14},{14,12},{1,3},{3,1},... | collective-permute-start | bytes 1572872 | tf_op jit(solution)/shard_map/ppermute | solution.py:67
  173.1 31.4 %collective-permute-start.22 = (bf16[512,512]{1,0:T(8,128)(2,1)S(1)}, bf16[512,512]{1,0:T(8,128)(2,1)}, u32[]{:S(2)}, u32[]{:S(2)}) collective-permute-start(bf16[512,512]{1,0:T(8,128)(2,1)S(1)} %piece.26), channel_id=1, source_target_pairs={{4,8},{6,10},{8,4},{10,6},{5,9},{7,11},{9,5},{11,7},{20,24},{22,26... | collective-permute-start | bytes 1572872 | tf_op jit(solution)/shard_map/ppermute | solution.py:60
  174.6 25.0 %collective-permute-start.23 = (bf16[512,512]{1,0:T(8,128)(2,1)S(1)}, bf16[512,512]{1,0:T(8,128)(2,1)}, u32[]{:S(2)}, u32[]{:S(2)}) collective-permute-start(bf16[512,512]{1,0:T(8,128)(2,1)S(1)} %piece.26), channel_id=1, source_target_pairs={{0,4},{2,6},{12,8},{14,10},{1,5},{3,7},{13,9},{15,11},{16,20},{18,... | collective-permute-start | bytes 1572872 | tf_op jit(solution)/shard_map/ppermute | solution.py:60
  186.4 15.1 %collective-permute-start.14 = (bf16[512,512]{1,0:T(8,128)(2,1)S(1)}, bf16[512,512]{1,0:T(8,128)(2,1)S(1)}, u32[]{:S(2)}, u32[]{:S(2)}) collective-permute-start(bf16[512,512]{1,0:T(8,128)(2,1)S(1)} %piece.19), channel_id=1, source_target_pairs={{0,2},{2,0},{4,6},{6,4},{8,10},{10,8},{12,14},{14,12},{1,3},{3,1},... | collective-permute-start | bytes 1572872 | tf_op jit(solution)/shard_map/ppermute | solution.py:67
  190.0 13.6 %collective-permute-start.17 = (bf16[512,512]{1,0:T(8,128)(2,1)S(1)}, bf16[512,512]{1,0:T(8,128)(2,1)S(1)}, u32[]{:S(2)}, u32[]{:S(2)}) collective-permute-start(bf16[512,512]{1,0:T(8,128)(2,1)S(1)} %add_convert_fusion.8), channel_id=1, source_target_pairs={{0,4},{2,6},{12,8},{14,10},{1,5},{3,7},{13,9},{15,11},{16,20},{18,... | collective-permute-start | bytes 1572872 | tf_op jit(solution)/shard_map/ppermute | solution.py:60
  192.4 22.4 %collective-permute-start.27 = (bf16[512,512]{1,0:T(8,128)(2,1)S(1)}, bf16[512,512]{1,0:T(8,128)(2,1)S(1)}, u32[]{:S(2)}, u32[]{:S(2)}) collective-permute-start(bf16[512,512]{1,0:T(8,128)(2,1)S(1)} %piece.31), channel_id=1, source_target_pairs={{0,4},{2,6},{12,8},{14,10},{1,5},{3,7},{13,9},{15,11},{16,20},{18,... | collective-permute-start | bytes 1572872 | tf_op jit(solution)/shard_map/ppermute | solution.py:60
  200.9 14.9 %collective-permute-start.24 = (bf16[512,512]{1,0:T(8,128)(2,1)S(1)}, bf16[512,512]{1,0:T(8,128)(2,1)S(1)}, u32[]{:S(2)}, u32[]{:S(2)}) collective-permute-start(bf16[512,512]{1,0:T(8,128)(2,1)S(1)} %add_convert_fusion.3), channel_id=1, source_target_pairs={{0,2},{2,0},{4,6},{6,4},{8,10},{10,8},{12,14},{14,12},{1,3},{3,1},... | collective-permute-start | bytes 1572872 | tf_op jit(solution)/shard_map/ppermute | solution.py:67
  201.5 23.7 %collective-permute-start.15 = (bf16[512,512]{1,0:T(8,128)(2,1)S(1)}, bf16[512,512]{1,0:T(8,128)(2,1)S(1)}, u32[]{:S(2)}, u32[]{:S(2)}) collective-permute-start(bf16[512,512]{1,0:T(8,128)(2,1)S(1)} %piece.18), channel_id=1, source_target_pairs={{0,2},{2,0},{4,6},{6,4},{8,10},{10,8},{12,14},{14,12},{1,3},{3,1},... | collective-permute-start | bytes 1572872 | tf_op jit(solution)/shard_map/ppermute | solution.py:67
  203.9 22.1 %collective-permute-start.18 = (bf16[512,512]{1,0:T(8,128)(2,1)S(1)}, bf16[512,512]{1,0:T(8,128)(2,1)S(1)}, u32[]{:S(2)}, u32[]{:S(2)}) collective-permute-start(bf16[512,512]{1,0:T(8,128)(2,1)S(1)} %add_convert_fusion.7), channel_id=1, source_target_pairs={{4,8},{6,10},{8,4},{10,6},{5,9},{7,11},{9,5},{11,7},{20,24},{22,26... | collective-permute-start | bytes 1572872 | tf_op jit(solution)/shard_map/ppermute | solution.py:60
  205.8 21.7 %collective-permute-start.20 = (bf16[512,512]{1,0:T(8,128)(2,1)S(1)}, bf16[512,512]{1,0:T(8,128)(2,1)S(1)}, u32[]{:S(2)}, u32[]{:S(2)}) collective-permute-start(bf16[512,512]{1,0:T(8,128)(2,1)S(1)} %add_convert_fusion.7), channel_id=1, source_target_pairs={{0,4},{2,6},{12,8},{14,10},{1,5},{3,7},{13,9},{15,11},{16,20},{18,... | collective-permute-start | bytes 1572872 | tf_op jit(solution)/shard_map/ppermute | solution.py:60
  216.1 25.5 %collective-permute-start.28 = (bf16[512,512]{1,0:T(8,128)(2,1)S(1)}, bf16[512,512]{1,0:T(8,128)(2,1)S(1)}, u32[]{:S(2)}, u32[]{:S(2)}) collective-permute-start(bf16[512,512]{1,0:T(8,128)(2,1)S(1)} %add_convert_fusion.2), channel_id=1, source_target_pairs={{4,8},{6,10},{8,4},{10,6},{5,9},{7,11},{9,5},{11,7},{20,24},{22,26... | collective-permute-start | bytes 1572872 | tf_op jit(solution)/shard_map/ppermute | solution.py:60
  216.8 26.6 %collective-permute-start.30 = (bf16[512,512]{1,0:T(8,128)(2,1)S(1)}, bf16[512,512]{1,0:T(8,128)(2,1)S(1)}, u32[]{:S(2)}, u32[]{:S(2)}) collective-permute-start(bf16[512,512]{1,0:T(8,128)(2,1)S(1)} %add_convert_fusion.2), channel_id=1, source_target_pairs={{0,4},{2,6},{12,8},{14,10},{1,5},{3,7},{13,9},{15,11},{16,20},{18,... | collective-permute-start | bytes 1572872 | tf_op jit(solution)/shard_map/ppermute | solution.py:60
  225.3 14.9 %collective-permute-start.25 = (bf16[512,512]{1,0:T(8,128)(2,1)S(1)}, bf16[512,512]{1,0:T(8,128)(2,1)S(1)}, u32[]{:S(2)}, u32[]{:S(2)}) collective-permute-start(bf16[512,512]{1,0:T(8,128)(2,1)S(1)} %piece.27), channel_id=1, source_target_pairs={{0,2},{2,0},{4,6},{6,4},{8,10},{10,8},{12,14},{14,12},{1,3},{3,1},... | collective-permute-start | bytes 1572872 | tf_op jit(solution)/shard_map/ppermute | solution.py:67
  225.9 25.4 %collective-permute-start.16 = (bf16[512,512]{1,0:T(8,128)(2,1)S(1)}, bf16[512,512]{1,0:T(8,128)(2,1)S(1)}, u32[]{:S(2)}, u32[]{:S(2)}) collective-permute-start(bf16[512,512]{1,0:T(8,128)(2,1)S(1)} %piece.17), channel_id=1, source_target_pairs={{0,2},{2,0},{4,6},{6,4},{8,10},{10,8},{12,14},{14,12},{1,3},{3,1},... | collective-permute-start | bytes 1572872 | tf_op jit(solution)/shard_map/ppermute | solution.py:67
  227.5 32.6 %collective-permute-start.19 = (bf16[512,512]{1,0:T(8,128)(2,1)S(1)}, bf16[512,512]{1,0:T(8,128)(2,1)}, u32[]{:S(2)}, u32[]{:S(2)}) collective-permute-start(bf16[512,512]{1,0:T(8,128)(2,1)S(1)} %add_convert_fusion.6), channel_id=1, source_target_pairs={{0,4},{2,6},{4,0},{6,2},{8,12},{10,14},{12,8},{14,10},{1,5},{3,7},... | collective-permute-start | bytes 1572872 | tf_op jit(solution)/shard_map/ppermute | solution.py:60
  240.1 20.0 %collective-permute-start.21 = (bf16[512,512]{1,0:T(8,128)(2,1)}, bf16[512,512]{1,0:T(8,128)(2,1)}, u32[]{:S(2)}, u32[]{:S(2)}) collective-permute-start(bf16[512,512]{1,0:T(8,128)(2,1)} %add_convert_fusion.5), channel_id=1, source_target_pairs={{4,8},{6,10},{8,4},{10,6},{5,9},{7,11},{9,5},{11,7},{20,24},{22,26... | collective-permute-start | bytes 1572872 | tf_op jit(solution)/shard_map/ppermute | solution.py:60
  241.6 20.2 %collective-permute-start.26 = (bf16[512,512]{1,0:T(8,128)(2,1)S(1)}, bf16[512,512]{1,0:T(8,128)(2,1)}, u32[]{:S(2)}, u32[]{:S(2)}) collective-permute-start(bf16[512,512]{1,0:T(8,128)(2,1)S(1)} %add_convert_fusion.4), channel_id=1, source_target_pairs={{0,2},{2,0},{4,6},{6,4},{8,10},{10,8},{12,14},{14,12},{1,3},{3,1},... | collective-permute-start | bytes 1572872 | tf_op jit(solution)/shard_map/ppermute | solution.py:67
  243.3 18.4 %collective-permute-start.29 = (bf16[512,512]{1,0:T(8,128)(2,1)}, bf16[512,512]{1,0:T(8,128)(2,1)}, u32[]{:S(2)}, u32[]{:S(2)}) collective-permute-start(bf16[512,512]{1,0:T(8,128)(2,1)} %add_convert_fusion.1), channel_id=1, source_target_pairs={{0,4},{2,6},{4,0},{6,2},{8,12},{10,14},{12,8},{14,10},{1,5},{3,7},... | collective-permute-start | bytes 1572872 | tf_op jit(solution)/shard_map/ppermute | solution.py:60
  251.4 10.4 %collective-permute-start.31 = (bf16[512,512]{1,0:T(8,128)(2,1)}, bf16[512,512]{1,0:T(8,128)(2,1)S(1)}, u32[]{:S(2)}, u32[]{:S(2)}) collective-permute-start(bf16[512,512]{1,0:T(8,128)(2,1)} %add_convert_fusion), channel_id=1, source_target_pairs={{4,8},{6,10},{8,4},{10,6},{5,9},{7,11},{9,5},{11,7},{20,24},{22,26... | collective-permute-start | bytes 1572872 | tf_op jit(solution)/shard_map/ppermute | solution.py:60
  (18 other events, 103.6 us)
